TPU v7x, 512 devices: a whole 4x8x8 slice. The times are simulated.
512 devices in a mesh: row: 64 (over z_hi, y, core), key: 8 (over z_lo, x).
Axes of the slice: x: 4, y: 8, z: 8 (z_hi: 4, z_lo: 2; z = z_hi * 2 + z_lo), core: 2. Of those that a mesh axis runs over, the one named last changes fastest.
Arguments:
- queries: bfloat16 [256, 1024, 128], P('row', 'key'), may hold values from -28 to 28
- keys_in: bfloat16 [256, 1024, 128], P('row', 'key'), may hold values from -28 to 28
- values: bfloat16 [256, 1024, 128], P('row', 'key'), may hold values from -6 to 6
- cotangent: bfloat16 [256, 1024, 128], P('row', 'key'), may hold values from -48 to 48
- pair_bias: bfloat16 [4, 1024, 1024], P(None, ('key', 'row')), may hold values from -6 to 6
- key_lengths: int32 [256], P('row'), may hold values from 256 to 1024
Outputs:
- grad_queries: bfloat16 [256, 1024, 128], P('row', 'key')
- grad_keys: bfloat16 [256, 1024, 128], P('row', 'key')
- grad_values: bfloat16 [256, 1024, 128], P('row', 'key')
- grad_bias: float32 [4, 1024, 1024], P(None, ('key', 'row'))
All inputs are finite; a program needn't handle non-finite values.
Results may differ from a plain program's by a relative error of at most 0.035.
Values may be sent and summed in bfloat16 or wider, within the bound.
A program may use at most 64 MiB of HBM per device.

v0:
```python
import math

import jax
import jax.numpy as jnp
from jax import lax
from jax.sharding import PartitionSpec as P


def per_device(queries, keys_in, values, cotangent, pair_bias, key_lengths):
    rows_dev, block_len, feature = queries.shape
    head_count = pair_bias.shape[0]
    length = pair_bias.shape[2]
    head_dim = feature // head_count
    factor = 1.0 / math.sqrt(head_dim)
    key_count = lax.axis_size("key")
    bias_rows = lax.all_gather(pair_bias, "row", axis=1, tiled=True)
    bias_float = bias_rows.astype(jnp.float32)
    rows_step = 1
    step_count = rows_dev // rows_step
    key_pos = jnp.arange(length, dtype=jnp.int32)

    def regroup(array):
        return array.reshape((step_count, rows_step) + array.shape[1:])

    def one_step(bias_total, inputs):
        query_rows, key_rows, value_rows, grad_rows, lengths = inputs
        key_full, value_full = (
            lax.all_gather(key_rows, "key", axis=1, tiled=True),
            lax.all_gather(value_rows, "key", axis=1, tiled=True),
        )
        query_heads = query_rows.reshape(rows_step, block_len, head_count, head_dim)
        key_heads = key_full.reshape(rows_step, length, head_count, head_dim)
        value_heads = value_full.reshape(rows_step, length, head_count, head_dim)
        grad_heads = grad_rows.reshape(rows_step, block_len, head_count, head_dim)
        scores = (
            jnp.einsum(
                "gjhd,gkhd->ghjk", query_heads, key_heads, preferred_element_type=jnp.float32
            )
            * factor
            + bias_float[None]
        )
        usable = key_pos[None, :] < lengths[:, None]
        scores = jnp.where(usable[:, None, None, :], scores, -1e30)
        row_max = jnp.max(scores, axis=-1, keepdims=True)
        log_total = row_max + jnp.log(jnp.sum(jnp.exp(scores - row_max), axis=-1, keepdims=True))
        weights = jnp.exp(scores - log_total)
        weights_low = weights.astype(jnp.bfloat16)
        attended = jnp.einsum(
            "ghjk,gkhd->gjhd", weights_low, value_heads, preferred_element_type=jnp.float32
        )
        row_dot = jnp.transpose(
            jnp.sum(grad_heads.astype(jnp.float32) * attended, axis=-1), (0, 2, 1)
        )
        grad_weights = jnp.einsum(
            "gjhd,gkhd->ghjk", grad_heads, value_heads, preferred_element_type=jnp.float32
        )
        grad_scores = weights * (grad_weights - row_dot[..., None])
        grad_low = grad_scores.astype(jnp.bfloat16)
        grad_query = (
            jnp.einsum("ghjk,gkhd->gjhd", grad_low, key_heads, preferred_element_type=jnp.float32)
            * factor
        ).astype(jnp.bfloat16)
        key_part = (
            jnp.einsum("ghjk,gjhd->gkhd", grad_low, query_heads, preferred_element_type=jnp.float32)
            * factor
        ).astype(jnp.bfloat16)
        value_part = jnp.einsum(
            "ghjk,gjhd->gkhd", weights_low, grad_heads, preferred_element_type=jnp.float32
        ).astype(jnp.bfloat16)
        key_part = key_part.reshape(rows_step, length, feature)
        value_part = value_part.reshape(rows_step, length, feature)
        key_recv, value_recv = (
            lax.all_to_all(key_part, "key", split_axis=1, concat_axis=0, tiled=True),
            lax.all_to_all(value_part, "key", split_axis=1, concat_axis=0, tiled=True),
        )
        grad_key = jnp.sum(
            key_recv.reshape(key_count, rows_step, block_len, feature).astype(jnp.float32), axis=0
        ).astype(jnp.bfloat16)
        grad_value = jnp.sum(
            value_recv.reshape(key_count, rows_step, block_len, feature).astype(jnp.float32), axis=0
        ).astype(jnp.bfloat16)
        bias_total = bias_total + jnp.sum(grad_scores, axis=0)
        return (
            bias_total,
            (grad_query.reshape(rows_step, block_len, feature), grad_key, grad_value),
        )

    start_total = jnp.zeros((head_count, block_len, length), jnp.float32)
    bias_total, results = lax.scan(
        one_step,
        start_total,
        (
            regroup(queries),
            regroup(keys_in),
            regroup(values),
            regroup(cotangent),
            regroup(key_lengths),
        ),
    )
    grad_queries = results[0].reshape(rows_dev, block_len, feature)
    grad_keys = results[1].reshape(rows_dev, block_len, feature)
    grad_values = results[2].reshape(rows_dev, block_len, feature)
    summed = lax.psum(bias_total, "row")
    owned = block_len // lax.axis_size("row")
    grad_bias = lax.dynamic_slice_in_dim(summed, lax.axis_index("row") * owned, owned, 1)
    return (grad_queries, grad_keys, grad_values, grad_bias)


def solution(mesh):
    placed = (
        P("row", "key", None),
        P("row", "key", None),
        P("row", "key", None),
        P("row", "key", None),
        P(None, ("key", "row"), None),
        P("row"),
    )
    return jax.shard_map(
        per_device,
        mesh=mesh,
        in_specs=placed,
        out_specs=(
            P("row", "key", None),
            P("row", "key", None),
            P("row", "key", None),
            P(None, ("key", "row"), None),
        ),
        check_vma=False,
    )
```

profile of v0, /device:TPU:1, one launch (start us, length us, event | category | flops | bytes accessed | tf_op | source)
XLA Modules:
  0.0 1022.3 jit_solution(14416105836772987919)
XLA Ops:
  14.0 86.6 %all-gather.10.cloned.1.call-done = bf16[4,128,1024]{2,0,1:T(4,128)(2,1)} async-done(((bf16[4,2,1024]{2,0,1:T(4,128)(2,1)}), bf16[4,128,1024]{2,0,1:T(4,128)(2,1)}) %all-gather.10.cloned.1.call-update) | async-done | bytes 1048592 | tf_op jit(solution)/shard_map/all_gather | solution.py:16
  103.6 312.4 %while.20 = (s32[]{:T(128)}, f32[4,128,1024]{2,1,0:T(8,128)}, bf16[4,1,128,128]{3,2,0,1:T(8,128)(2,1)}, bf16[4,1,128,128]{3,2,0,1:T(8,128)(2,1)}, bf16[4,1,128,1...) while((s32[]{:T(128)}, f32[4,128,1024]{2,1,0:T(8,128)}, ...), condition=%wide.region_6.7_spmd.clone, body=%wide.region_0.6_spmd.clone.sunk | while | flops 210419712 | bytes 34693576 | solution.py:89
  104.4 20.2 %all-gather.7 = bf16[1,1,1024,128]{2,3,1,0:T(8,128)(2,1)S(1)} all-gather(bf16[1,1,128,128]{2,3,1,0:T(8,128)(2,1)S(1)} %constant_dynamic-slice_fusion.13), channel_id=2, replica_groups=mesh['row'=64,'key'=8] {'key'}, dimensions={2}, use_global_device_ids=true | all-gather | bytes 294912 | tf_op jit(solution)/shard_map/while/body/eval_jaxpr/all_gather | solution.py:28
  129.3 20.1 %all-gather.6 = bf16[1,1,1024,128]{2,3,1,0:T(8,128)(2,1)S(1)} all-gather(bf16[1,1,128,128]{2,3,1,0:T(8,128)(2,1)S(1)} %constant_dynamic-slice_fusion.11), channel_id=3, replica_groups=mesh['row'=64,'key'=8] {'key'}, dimensions={2}, use_global_device_ids=true | all-gather | bytes 294912 | tf_op jit(solution)/shard_map/while/body/eval_jaxpr/all_gather | solution.py:29
  157.8 4.0 all-to-all-start
  168.0 5.0 all-to-all-start.1
  175.2 3.9 all-to-all-done.1
  181.7 19.9 %all-gather.7 = bf16[1,1,1024,128]{2,3,1,0:T(8,128)(2,1)S(1)} all-gather(bf16[1,1,128,128]{2,3,1,0:T(8,128)(2,1)S(1)} %constant_dynamic-slice_fusion.13), channel_id=2, replica_groups=mesh['row'=64,'key'=8] {'key'}, dimensions={2}, use_global_device_ids=true | all-gather | bytes 294912 | tf_op jit(solution)/shard_map/while/body/eval_jaxpr/all_gather | solution.py:28
  206.3 19.6 %all-gather.6 = bf16[1,1,1024,128]{2,3,1,0:T(8,128)(2,1)S(1)} all-gather(bf16[1,1,128,128]{2,3,1,0:T(8,128)(2,1)S(1)} %constant_dynamic-slice_fusion.11), channel_id=3, replica_groups=mesh['row'=64,'key'=8] {'key'}, dimensions={2}, use_global_device_ids=true | all-gather | bytes 294912 | tf_op jit(solution)/shard_map/while/body/eval_jaxpr/all_gather | solution.py:29
  226.5 3.6 select_add_fusion.2
  235.9 4.0 all-to-all-start
  246.1 5.0 all-to-all-start.1
  253.3 3.9 all-to-all-done.1
  259.8 20.4 %all-gather.7 = bf16[1,1,1024,128]{2,3,1,0:T(8,128)(2,1)S(1)} all-gather(bf16[1,1,128,128]{2,3,1,0:T(8,128)(2,1)S(1)} %constant_dynamic-slice_fusion.13), channel_id=2, replica_groups=mesh['row'=64,'key'=8] {'key'}, dimensions={2}, use_global_device_ids=true | all-gather | bytes 294912 | tf_op jit(solution)/shard_map/while/body/eval_jaxpr/all_gather | solution.py:28
  285.0 20.0 %all-gather.6 = bf16[1,1,1024,128]{2,3,1,0:T(8,128)(2,1)S(1)} all-gather(bf16[1,1,128,128]{2,3,1,0:T(8,128)(2,1)S(1)} %constant_dynamic-slice_fusion.11), channel_id=3, replica_groups=mesh['row'=64,'key'=8] {'key'}, dimensions={2}, use_global_device_ids=true | all-gather | bytes 294912 | tf_op jit(solution)/shard_map/while/body/eval_jaxpr/all_gather | solution.py:29
  315.0 4.0 all-to-all-start
  325.1 5.0 all-to-all-start.1
  332.3 3.9 all-to-all-done.1
  338.9 19.7 %all-gather.7 = bf16[1,1,1024,128]{2,3,1,0:T(8,128)(2,1)S(1)} all-gather(bf16[1,1,128,128]{2,3,1,0:T(8,128)(2,1)S(1)} %constant_dynamic-slice_fusion.13), channel_id=2, replica_groups=mesh['row'=64,'key'=8] {'key'}, dimensions={2}, use_global_device_ids=true | all-gather | bytes 294912 | tf_op jit(solution)/shard_map/while/body/eval_jaxpr/all_gather | solution.py:28
  363.3 19.6 %all-gather.6 = bf16[1,1,1024,128]{2,3,1,0:T(8,128)(2,1)S(1)} all-gather(bf16[1,1,128,128]{2,3,1,0:T(8,128)(2,1)S(1)} %constant_dynamic-slice_fusion.11), channel_id=3, replica_groups=mesh['row'=64,'key'=8] {'key'}, dimensions={2}, use_global_device_ids=true | all-gather | bytes 294912 | tf_op jit(solution)/shard_map/while/body/eval_jaxpr/all_gather | solution.py:29
  392.9 4.0 all-to-all-start
  403.0 5.0 all-to-all-start.1
  410.2 4.0 all-to-all-done.1
  416.1 597.9 %all-reduce.2.cloned.1.call-done = f32[4,128,1024]{2,1,0:T(8,128)} async-done(((f32[4,128,1024]{2,1,0:T(8,128)}), f32[4,128,1024]{2,1,0:T(8,128)}) %all-reduce.2.cloned.1.call-update) | async-done | bytes 2097168 | tf_op jit(solution)/shard_map/psum | solution.py:103
  (208 shorter events, 107.9 us)
Async XLA Ops:
  7.2 93.5 %all-gather.10.cloned.1.call-start = ((), (), s32[]{:S(2)}) async-start(), calls=%async_computation.2 | async-start | bytes 1064960 | tf_op jit(solution)/shard_map/all_gather | solution.py:16
  8.6 1005.4 %all-reduce.2.cloned.1.call-start = ((), (), s32[]{:S(2)}) async-start(), calls=%async_computation.3 | async-start | bytes 4194304 | tf_op jit(solution)/shard_map/psum | solution.py:103
  8.7 95.0 %copy-start.6 = (s32[4]{0:T(128)S(1)}, s32[4]{0:T(128)}, u32[]{:S(2)}) copy-start(s32[4]{0:T(128)} %param.13) | copy-start | bytes 52
  103.6 25.7 %copy-start.4 = (bf16[4,1,128,128]{2,3,1,0:T(8,128)(2,1)}, bf16[4,1,128,128]{2,3,1,0:T(8,128)(2,1)S(1)}, u32[]{:S(2)}) copy-start(bf16[4,1,128,128]{2,3,1,0:T(8,128)(2,1)S(1)} %get-tuple-element.412) | copy-start | bytes 393220 | tf_op jit(solution)/shard_map/while
  103.6 45.8 %copy-start.2 = (bf16[4,1,128,128]{2,3,1,0:T(8,128)(2,1)}, bf16[4,1,128,128]{2,3,1,0:T(8,128)(2,1)S(1)}, u32[]{:S(2)}) copy-start(bf16[4,1,128,128]{2,3,1,0:T(8,128)(2,1)S(1)} %get-tuple-element.411) | copy-start | bytes 393220 | tf_op jit(solution)/shard_map/while
  157.8 10.1 all-to-all-start
  161.9 11.1 %copy-start.1 = (bf16[1,1,1024,128]{2,3,1,0:T(8,128)(2,1)S(1)}, bf16[1,1,1024,128]{2,3,1,0:T(8,128)(2,1)}, u32[]{:S(2)}) copy-start(bf16[1,1,1024,128]{2,3,1,0:T(8,128)(2,1)} %copy-done) | copy-start | bytes 786436 | tf_op jit(solution)/shard_map/while
  168.0 11.1 %all-to-all-start.1 = ((bf16[8,2,8192]{2,1,0:T(2,128)(2,1)}), bf16[8,2,8192]{2,1,0:T(2,128)(2,1)S(1)}, u32[]{:S(2)}, u32[]{:S(2)}) async-start(bf16[8,2,8192]{2,1,0:T(2,128)(2,1)} %reshape.260), calls=%async_computation.1 | async-start | bytes 524288 | tf_op jit(solution)/shard_map/while/body/eval_jaxpr/all_to_all | solution.py:74
  180.9 25.4 %copy-start.4 = (bf16[4,1,128,128]{2,3,1,0:T(8,128)(2,1)}, bf16[4,1,128,128]{2,3,1,0:T(8,128)(2,1)S(1)}, u32[]{:S(2)}) copy-start(bf16[4,1,128,128]{2,3,1,0:T(8,128)(2,1)S(1)} %get-tuple-element.412) | copy-start | bytes 393220 | tf_op jit(solution)/shard_map/while
  180.9 45.0 %copy-start.2 = (bf16[4,1,128,128]{2,3,1,0:T(8,128)(2,1)}, bf16[4,1,128,128]{2,3,1,0:T(8,128)(2,1)S(1)}, u32[]{:S(2)}) copy-start(bf16[4,1,128,128]{2,3,1,0:T(8,128)(2,1)S(1)} %get-tuple-element.411) | copy-start | bytes 393220 | tf_op jit(solution)/shard_map/while
  235.9 10.1 all-to-all-start
  240.0 11.1 %copy-start.1 = (bf16[1,1,1024,128]{2,3,1,0:T(8,128)(2,1)S(1)}, bf16[1,1,1024,128]{2,3,1,0:T(8,128)(2,1)}, u32[]{:S(2)}) copy-start(bf16[1,1,1024,128]{2,3,1,0:T(8,128)(2,1)} %copy-done) | copy-start | bytes 786436 | tf_op jit(solution)/shard_map/while
  246.1 11.1 %all-to-all-start.1 = ((bf16[8,2,8192]{2,1,0:T(2,128)(2,1)}), bf16[8,2,8192]{2,1,0:T(2,128)(2,1)S(1)}, u32[]{:S(2)}, u32[]{:S(2)}) async-start(bf16[8,2,8192]{2,1,0:T(2,128)(2,1)} %reshape.260), calls=%async_computation.1 | async-start | bytes 524288 | tf_op jit(solution)/shard_map/while/body/eval_jaxpr/all_to_all | solution.py:74
  259.1 25.9 %copy-start.4 = (bf16[4,1,128,128]{2,3,1,0:T(8,128)(2,1)}, bf16[4,1,128,128]{2,3,1,0:T(8,128)(2,1)S(1)}, u32[]{:S(2)}) copy-start(bf16[4,1,128,128]{2,3,1,0:T(8,128)(2,1)S(1)} %get-tuple-element.412) | copy-start | bytes 393220 | tf_op jit(solution)/shard_map/while
  259.1 45.9 %copy-start.2 = (bf16[4,1,128,128]{2,3,1,0:T(8,128)(2,1)}, bf16[4,1,128,128]{2,3,1,0:T(8,128)(2,1)S(1)}, u32[]{:S(2)}) copy-start(bf16[4,1,128,128]{2,3,1,0:T(8,128)(2,1)S(1)} %get-tuple-element.411) | copy-start | bytes 393220 | tf_op jit(solution)/shard_map/while
  315.0 10.1 all-to-all-start
  319.0 11.1 %copy-start.1 = (bf16[1,1,1024,128]{2,3,1,0:T(8,128)(2,1)S(1)}, bf16[1,1,1024,128]{2,3,1,0:T(8,128)(2,1)}, u32[]{:S(2)}) copy-start(bf16[1,1,1024,128]{2,3,1,0:T(8,128)(2,1)} %copy-done) | copy-start | bytes 786436 | tf_op jit(solution)/shard_map/while
  325.1 11.1 %all-to-all-start.1 = ((bf16[8,2,8192]{2,1,0:T(2,128)(2,1)}), bf16[8,2,8192]{2,1,0:T(2,128)(2,1)S(1)}, u32[]{:S(2)}, u32[]{:S(2)}) async-start(bf16[8,2,8192]{2,1,0:T(2,128)(2,1)} %reshape.260), calls=%async_computation.1 | async-start | bytes 524288 | tf_op jit(solution)/shard_map/while/body/eval_jaxpr/all_to_all | solution.py:74
  338.1 25.2 %copy-start.4 = (bf16[4,1,128,128]{2,3,1,0:T(8,128)(2,1)}, bf16[4,1,128,128]{2,3,1,0:T(8,128)(2,1)S(1)}, u32[]{:S(2)}) copy-start(bf16[4,1,128,128]{2,3,1,0:T(8,128)(2,1)S(1)} %get-tuple-element.412) | copy-start | bytes 393220 | tf_op jit(solution)/shard_map/while
  338.1 44.9 %copy-start.2 = (bf16[4,1,128,128]{2,3,1,0:T(8,128)(2,1)}, bf16[4,1,128,128]{2,3,1,0:T(8,128)(2,1)S(1)}, u32[]{:S(2)}) copy-start(bf16[4,1,128,128]{2,3,1,0:T(8,128)(2,1)S(1)} %get-tuple-element.411) | copy-start | bytes 393220 | tf_op jit(solution)/shard_map/while
  392.9 10.1 all-to-all-start
  397.0 11.1 %copy-start.1 = (bf16[1,1,1024,128]{2,3,1,0:T(8,128)(2,1)S(1)}, bf16[1,1,1024,128]{2,3,1,0:T(8,128)(2,1)}, u32[]{:S(2)}) copy-start(bf16[1,1,1024,128]{2,3,1,0:T(8,128)(2,1)} %copy-done) | copy-start | bytes 786436 | tf_op jit(solution)/shard_map/while
  403.0 11.1 %all-to-all-start.1 = ((bf16[8,2,8192]{2,1,0:T(2,128)(2,1)}), bf16[8,2,8192]{2,1,0:T(2,128)(2,1)S(1)}, u32[]{:S(2)}, u32[]{:S(2)}) async-start(bf16[8,2,8192]{2,1,0:T(2,128)(2,1)} %reshape.260), calls=%async_computation.1 | async-start | bytes 524288 | tf_op jit(solution)/shard_map/while/body/eval_jaxpr/all_to_all | solution.py:74
  408.7 7.4 copy-start.3
  (11 other events, 68.3 us)
Sparse Core Ops, SparseCore 0:
  11.9 88.7 all-gather.9
  416.2 597.7 all-reduce.1
where the time goes:
time: 1020 us
  waiting for transfers between devices  700 us (69%)
  blocking collectives  160 us (16%)
  local copies, waits for them, and re-layouts  53.2 us (5%)
  starting transfers between devices  36.3 us (4%)
  matrix products  32 us (3%)
  other arithmetic  26.2 us (3%)
  between operations  14.1 us (1%)
    psum x1, waiting for transfers between devices, per_device(): summed = lax.psum(bias_total, 'row')  598 us
    all_gather x1, waiting for transfers between devices, per_device(): bias_rows = lax.all_gather(pair_bias, 'row', axis=1, tiled=True)  86.6 us
    all_gather x4, blocking collectives, one_step(): lax.all_gather(key_rows, 'key', axis=1, tiled=True)  80.2 us
    all_gather x4, blocking collectives, one_step(): lax.all_gather(value_rows, 'key', axis=1, tiled=True)  79.4 us
    while x8, other arithmetic  21.4 us
  transfers between devices with their start and end apart: 10, of which 6 were waited for; matrix products, arithmetic and copies ran while one was open for 4% of the time, Pallas kernels for 0%

commit v1 on v0

v1 whole, which is shorter than its diff:
```python
import math

import jax
import jax.numpy as jnp
from jax import lax
from jax.experimental import pallas as pl
from jax.experimental.pallas import tpu as pltpu
from jax.sharding import PartitionSpec as P

MESH = pl.DeviceIdType.MESH
VM = pltpu.VMEM
BF = jnp.bfloat16
F32 = jnp.float32
NX, NA = 4, 2
NY, NC = 8, 2
LOG2E = 1.4426950408889634


def place():
    row, key = lax.axis_index("row"), lax.axis_index("key")
    return (
        row,
        key,
        lax.div(key, NX),
        lax.rem(key, NX),
        lax.div(row, NY * NC),
        lax.rem(lax.div(row, NC), NY),
        lax.rem(row, NC),
    )


def row_of(z, y, core):
    return (z * NY + y) * NC + core


def greet(nz):
    row, key, a, x, z, y, core = place()
    barrier = pltpu.get_barrier_semaphore()
    peers = [(row, lax.rem(key + s, NA * NX)) for s in range(1, NA * NX)]
    peers += [(row_of(lax.rem(z + s, nz), y, core), key) for s in range(1, nz)]
    peers += [(row_of(z, lax.rem(y + s, NY), core), key) for s in range(1, NY)]
    peers += [(row_of(z, y, 1 - core), key)]
    for peer in peers:
        pl.semaphore_signal(barrier, inc=1, device_id=peer, device_id_type=MESH)
    pl.semaphore_wait(barrier, len(peers))


def remote(src, dst, send, recv, index, peer):
    return pltpu.make_async_remote_copy(
        src_ref=src,
        dst_ref=dst,
        send_sem=send.at[index],
        recv_sem=recv.at[index],
        device_id=peer,
        device_id_type=MESH,
    )


def gather_kernel(
    nz, q, k, v, c, bias, kv, qc, bg, own, kvs, qcs,
    s0, r0, s1a, r1a, s1b, r1b, s2a, r2a, s2b, r2b, s3, r3, skv, rkv, sqc, rqc, loc,
):
    row, key, a, x, z, y, core = place()
    rows_dev = q.shape[0]
    dim = q.shape[2] // NX
    greet(nz)
    first = []
    for s in range(1, NX):
        to = lax.rem(x + s, NX)
        cp = remote(bias.at[to], own.at[x], s0, r0, s - 1, (row, a * NX + to))
        cp.start()
        first.append(cp)
    own[x] = bias[x]
    for part, source in enumerate((k, v)):
        for i in range(rows_dev):
            turned = source[i].T
            for h in range(NX):
                kvs[h, part, i] = turned[h * dim : (h + 1) * dim]
    for cp in first:
        cp.wait()
    bg[z, y, core] = own[...]
    phase1a, phase1b = [], []
    for s in range(1, nz):
        cp = remote(
            own.at[0:2], bg.at[z, y, core, 0:2], s1a, r1a, s - 1,
            (row_of(lax.rem(z + s, nz), y, core), key),
        )
        cp.start()
        phase1a.append(cp)
    for s in range(1, NY):
        cp = remote(
            own.at[2:4], bg.at[z, y, core, 2:4], s1b, r1b, s - 1,
            (row_of(z, lax.rem(y + s, NY), core), key),
        )
        cp.start()
        phase1b.append(cp)
    others = []
    for s in range(1, NA * NX):
        to = lax.rem(key + s, NA * NX)
        cp = remote(
            kvs.at[lax.rem(to, NX)], kv.at[:, :, :, pl.ds(key * 128, 128)],
            skv, rkv, s - 1, (row, to),
        )
        cp.start()
        others.append(cp)
    for part, source in enumerate((q, c)):
        for i in range(rows_dev):
            turned = source[i].T
            for h in range(NX):
                qcs[h, part, i] = turned[h * dim : (h + 1) * dim]
    for s in range(1, NX):
        to = lax.rem(x + s, NX)
        cp = remote(
            qcs.at[to], qc.at[:, :, :, pl.ds(x * 128, 128)],
            sqc, rqc, s - 1, (row, a * NX + to),
        )
        cp.start()
        others.append(cp)
    mine = [
        pltpu.make_async_copy(kvs.at[x], kv.at[:, :, :, pl.ds(key * 128, 128)], loc.at[0]),
        pltpu.make_async_copy(qcs.at[x], qc.at[:, :, :, pl.ds(x * 128, 128)], loc.at[1]),
    ]
    for cp in mine:
        cp.start()
    for cp in phase1a:
        cp.wait()
    phase2a, phase2b = [], []
    for s in range(1, NY):
        cp = remote(
            bg.at[:, y, core, 0:2], bg.at[:, y, core, 0:2], s2a, r2a, s - 1,
            (row_of(z, lax.rem(y + s, NY), core), key),
        )
        cp.start()
        phase2a.append(cp)
    for cp in phase1b:
        cp.wait()
    for s in range(1, nz):
        cp = remote(
            bg.at[z, :, core, 2:4], bg.at[z, :, core, 2:4], s2b, r2b, s - 1,
            (row_of(lax.rem(z + s, nz), y, core), key),
        )
        cp.start()
        phase2b.append(cp)
    partner = (row_of(z, y, 1 - core), key)
    phase3 = []
    for s in range(NY):
        if s:
            phase2a[s - 1].wait()
        at = lax.rem(y + NY - s, NY)
        cp = remote(
            bg.at[:, at, core, 0:2], bg.at[:, at, core, 0:2], s3, r3, s, partner
        )
        cp.start()
        phase3.append(cp)
    for s in range(nz):
        if s:
            phase2b[s - 1].wait()
        at = lax.rem(z + nz - s, nz)
        cp = remote(
            bg.at[at, :, core, 2:4], bg.at[at, :, core, 2:4], s3, r3, NY + s, partner
        )
        cp.start()
        phase3.append(cp)
    for cp in mine + others + phase3:
        cp.wait()


def tile_kernel(nz, lengths, kv, qc, bg, dkv, gq, gb, q3, k3, cs, bias_f, total, stage, acc):
    rows_dev, dim, length = kv.shape[1:]
    mine = qc.shape[3]
    factor = 1.0 / math.sqrt(dim)
    tile = 128
    groups = NY * NC // 4

    def lay(n, carry):
        b, zz = n // nz, n % nz
        block = bg[zz, :, :, b].astype(F32) * LOG2E
        stage[...] = block.reshape(NY * NC * 16, 128)
        for g in range(groups):
            for t in range(8):
                j0 = pl.multiple_of(b * 128 + zz * (NY * NC * 2) + g * 8, 8)
                bias_f[pl.ds(j0, 8), t * 128 : (t + 1) * 128] = stage[
                    pl.ds(g * 64 + t, 8, stride=8), :
                ]
        return carry

    lax.fori_loop(0, 4 * nz, lay, 0)
    lane = lax.broadcasted_iota(jnp.int32, (16, length), 1)
    line = lax.broadcasted_iota(jnp.int32, (16, length), 0)
    for i in range(rows_dev):
        scaled = qc[0, i].astype(F32) * (factor * LOG2E)
        hi = scaled.astype(BF)
        rest = scaled - hi.astype(F32)
        mid = rest.astype(BF)
        low = (rest - mid.astype(F32)).astype(BF)
        ones = jnp.where(lax.broadcasted_iota(jnp.int32, (32, mine), 0) == 0, 1.0, 0.0).astype(BF)
        q3[i] = jnp.concatenate([hi, mid, low, ones], axis=0).T
        cs[i] = qc[1, i].T
        keys = kv[0, i]
        for n in range(3):
            k3[i, n * dim : (n + 1) * dim] = keys
        hidden = jnp.where((line == 0) & (lane >= lengths[i]), -1e30, 0.0).astype(BF)
        k3[i, 3 * dim : 3 * dim + 16] = hidden
        k3[i, 3 * dim + 16 :] = jnp.zeros((dim - 16, length), BF)
    acc[...] = jnp.zeros_like(acc)
    total[...] = jnp.zeros_like(total)

    def step(n, carry):
        jt, i = n // rows_dev, n % rows_dev
        rows = pl.ds(pl.multiple_of(jt * tile, tile), tile)
        s = jnp.dot(q3[i, rows], k3[i], preferred_element_type=F32) + bias_f[rows]
        p = jnp.exp2(s - jnp.max(s, axis=1, keepdims=True))
        w = p * (1.0 / jnp.sum(p, axis=1, keepdims=True))
        gw = jnp.dot(cs[i, rows], kv[1, i], preferred_element_type=F32)
        g = w * (gw - jnp.sum(w * gw, axis=1, keepdims=True))
        total[rows] += g
        gl = g.astype(BF)
        gq[i, :, rows] = (
            lax.dot_general(
                kv[0, i], gl, (((1,), (1,)), ((), ())), preferred_element_type=F32
            )
            * factor
        ).astype(BF)
        acc[0, i] += jnp.dot(qc[0, i, :, rows], gl, preferred_element_type=F32)
        acc[1, i] += jnp.dot(qc[1, i, :, rows], w.astype(BF), preferred_element_type=F32)
        return carry

    lax.fori_loop(0, rows_dev * (mine // tile), step, 0)
    for i in range(rows_dev):
        dkv[0, i] = (acc[0, i] * factor).astype(BF)
        dkv[1, i] = acc[1, i].astype(BF)

    def unlay(n, carry):
        b, zz = n // nz, n % nz
        for g in range(groups):
            for t in range(8):
                j0 = pl.multiple_of(b * 128 + zz * (NY * NC * 2) + g * 8, 8)
                stage[pl.ds(g * 64 + t, 8, stride=8), :] = total[
                    pl.ds(j0, 8), t * 128 : (t + 1) * 128
                ]
        gb[zz, :, :, b] = stage[...].reshape(NY, NC, 16, 128).astype(BF)
        return carry

    lax.fori_loop(0, 4 * nz, unlay, 0)


def scatter_kernel(
    nz, dkv, gq, gb, oq, ok, ov, ob, sum1, sum2a, sum2b, sum3, rk, rq, r1, r2a, r2b, r3a, r3b,
    s1, q1, s2a, q2a, s2b, q2b, s3a, q3a, s3b, q3b, s4, q4, skv, qkv, sq, qq, loc,
):
    row, key, a, x, z, y, core = place()
    rows_dev = dkv.shape[1]
    greet(nz)
    swap = remote(gb.at[:, :, 1 - core], r1, s1, q1, 0, (row_of(z, y, 1 - core), key))
    swap.start()
    others = []
    for s in range(1, NA * NX):
        to = lax.rem(key + s, NA * NX)
        cp = remote(
            dkv.at[:, :, :, pl.ds(to * 128, 128)], rk.at[key], skv, qkv, s - 1, (row, to)
        )
        cp.start()
        others.append(cp)
    for s in range(1, NX):
        to = lax.rem(x + s, NX)
        cp = remote(
            gq.at[:, :, pl.ds(to * 128, 128)], rq.at[x], sq, qq, s - 1, (row, a * NX + to)
        )
        cp.start()
        others.append(cp)
    mine = [
        pltpu.make_async_copy(dkv.at[:, :, :, pl.ds(key * 128, 128)], rk.at[key], loc.at[0]),
        pltpu.make_async_copy(gq.at[:, :, pl.ds(x * 128, 128)], rq.at[x], loc.at[1]),
    ]
    for cp in mine:
        cp.start()
    swap.wait()

    def join(n, carry):
        sum1[n] = (gb[n, :, core].astype(F32) + r1[n].astype(F32)).astype(BF)
        return carry

    lax.fori_loop(0, nz, join, 0)
    phase2a, phase2b = [], []
    for s in range(1, NY):
        to = lax.rem(y + s, NY)
        cp = remote(sum1.at[:, to, 0:2], r2a.at[s - 1], s2a, q2a, s - 1, (row_of(z, to, core), key))
        cp.start()
        phase2a.append(cp)
    for s in range(1, nz):
        to = lax.rem(z + s, nz)
        cp = remote(sum1.at[to, :, 2:4], r2b.at[s - 1], s2b, q2b, s - 1, (row_of(to, y, core), key))
        cp.start()
        phase2b.append(cp)
    phase3 = []
    for cp in phase2a:
        cp.wait()
    part = sum1[:, y, 0:2].astype(F32)
    for s in range(NY - 1):
        part += r2a[s].astype(F32)
    sum2a[...] = part.astype(BF)
    for s in range(1, nz):
        to = lax.rem(z + s, nz)
        cp = remote(sum2a.at[to], r3a.at[s - 1], s3a, q3a, s - 1, (row_of(to, y, core), key))
        cp.start()
        phase3.append(cp)
    for cp in phase2b:
        cp.wait()
    part = sum1[z, :, 2:4].astype(F32)
    for s in range(nz - 1):
        part += r2b[s].astype(F32)
    sum2b[...] = part.astype(BF)
    for s in range(1, NY):
        to = lax.rem(y + s, NY)
        cp = remote(sum2b.at[to], r3b.at[s - 1], s3b, q3b, s - 1, (row_of(z, to, core), key))
        cp.start()
        phase3.append(cp)
    for cp in phase3:
        cp.wait()
    part = sum2a[z].astype(F32)
    for s in range(nz - 1):
        part += r3a[s].astype(F32)
    sum3[0:2] = part
    part = sum2b[y].astype(F32)
    for s in range(NY - 1):
        part += r3b[s].astype(F32)
    sum3[2:4] = part
    last = []
    for s in range(1, NX):
        to = lax.rem(x + s, NX)
        cp = remote(sum3.at[to], ob.at[x], s4, q4, s - 1, (row, a * NX + to))
        cp.start()
        last.append(cp)
    ob[x] = sum3[x]
    for cp in mine + others:
        cp.wait()
    for i in range(rows_dev):
        oq[i] = jnp.concatenate([rq[h, i] for h in range(NX)], axis=0).T
        for part, out in enumerate((ok, ov)):
            both = [
                rk[h, part, i].astype(F32) + rk[NX + h, part, i].astype(F32) for h in range(NX)
            ]
            out[i] = jnp.concatenate(both, axis=0).astype(BF).T
    for cp in last:
        cp.wait()


def dma(*shape):
    return pltpu.SemaphoreType.DMA(shape)


def per_device(queries, keys_in, values, cotangent, pair_bias, key_lengths):
    rows_dev, block, feature = queries.shape
    heads, owned, length = pair_bias.shape
    dim = feature // heads
    nz = lax.axis_size("row") // (NY * NC)
    piece = (owned * length // 128, 128)
    mine = NX * block
    vmem = pl.BlockSpec(memory_space=VM)
    limit = 56 * 1024 * 1024
    kv_type = jax.ShapeDtypeStruct((2, rows_dev, dim, length), BF)
    qc_type = jax.ShapeDtypeStruct((2, rows_dev, dim, mine), BF)
    bg_type = jax.ShapeDtypeStruct((nz, NY, NC, NX) + piece, BF)

    def pairs(*counts):
        return [dma(n) for n in counts for _ in range(2)]

    kv, qc, bg = pl.pallas_call(
        lambda *refs: gather_kernel(nz, *refs),
        out_shape=(kv_type, qc_type, bg_type),
        in_specs=[vmem] * 5,
        out_specs=(vmem,) * 3,
        scratch_shapes=[
            VM((NX,) + piece, BF),
            VM((NX, 2, rows_dev, dim, block), BF),
            VM((NX, 2, rows_dev, dim, block), BF),
        ]
        + pairs(NX - 1, nz - 1, NY - 1, NY - 1, nz - 1, NY + nz, NA * NX - 1, NX - 1)
        + [dma(2)],
        compiler_params=pltpu.CompilerParams(
            collective_id=0, has_side_effects=True, vmem_limit_bytes=limit
        ),
        name="gather",
    )(queries, keys_in, values, cotangent, pair_bias.reshape((heads,) + piece))

    dkv, gq, gb = pl.pallas_call(
        lambda *refs: tile_kernel(nz, *refs),
        out_shape=(kv_type, jax.ShapeDtypeStruct((rows_dev, dim, mine), BF), bg_type),
        in_specs=[pl.BlockSpec(memory_space=pltpu.SMEM)] + [vmem] * 3,
        out_specs=(vmem,) * 3,
        scratch_shapes=[
            VM((rows_dev, mine, 4 * dim), BF),
            VM((rows_dev, 4 * dim, length), BF),
            VM((rows_dev, mine, dim), BF),
            VM((mine, length), F32),
            VM((mine, length), F32),
            VM((NY * NC * piece[0], 128), F32),
            VM((2, rows_dev, dim, length), F32),
        ],
        compiler_params=pltpu.CompilerParams(vmem_limit_bytes=limit),
        name="tiles",
    )(key_lengths, kv, qc, bg)

    kind = jax.ShapeDtypeStruct(queries.shape, BF)
    gq, gk, gv, gbias = pl.pallas_call(
        lambda *refs: scatter_kernel(nz, *refs),
        out_shape=(kind, kind, kind, jax.ShapeDtypeStruct((heads,) + piece, F32)),
        in_specs=[vmem] * 3,
        out_specs=(vmem,) * 4,
        scratch_shapes=[
            VM((nz, NY, NX) + piece, BF),
            VM((nz, 2) + piece, BF),
            VM((NY, 2) + piece, BF),
            VM((NX,) + piece, F32),
            VM((NA * NX, 2, rows_dev, dim, block), BF),
            VM((NX, rows_dev, dim, block), BF),
            VM((nz, NY, NX) + piece, BF),
            VM((NY - 1, nz, 2) + piece, BF),
            VM((nz - 1, NY, 2) + piece, BF),
            VM((nz - 1, 2) + piece, BF),
            VM((NY - 1, 2) + piece, BF),
        ]
        + pairs(1, NY - 1, nz - 1, nz - 1, NY - 1, NX - 1, NA * NX - 1, NX - 1)
        + [dma(2)],
        compiler_params=pltpu.CompilerParams(
            collective_id=1, has_side_effects=True, vmem_limit_bytes=limit
        ),
        name="scatter",
    )(dkv, gq, gb)
    return gq, gk, gv, gbias.reshape(pair_bias.shape)


def solution(mesh):
    wide = P("row", "key", None)
    bias = P(None, ("key", "row"), None)
    return jax.shard_map(
        per_device,
        mesh=mesh,
        in_specs=(wide, wide, wide, wide, bias, P("row")),
        out_specs=(wide, wide, wide, bias),
        check_vma=False,
    )
```

time: 1020 us -> 88.4 us (0.09)
  waiting for transfers between devices: 700 us -> 0 us
  blocking collectives: 160 us -> 0 us
  Pallas kernels: 0 us -> 80.4 us
  local copies, waits for them, and re-layouts: 53.2 us -> 5.94 us
  starting transfers between devices: 36.3 us -> 0 us
  matrix products: 32 us -> 0 us
  other arithmetic: 26.2 us -> 0 us
  between operations: 14.1 us -> 0.65 us
    psum x1 -> x0, waiting for transfers between devices: 598 us -> none  [per_device(): summed = lax.psum(bias_total, 'row')]
    all_gather x8 -> x0, blocking collectives: 160 us -> none  [the longest x4 80.2 us: one_step(): lax.all_gather(key_rows, 'key', axis=1, tiled=True)]
    all_gather x1 -> x0, waiting for transfers between devices: 86.6 us -> none  [per_device(): bias_rows = lax.all_gather(pair_bias, 'row', axis=1, tiled=True)]
    pallas_call x0 -> x3, Pallas kernels: none -> 80.4 us  [the longest x1 36.6 us: per_device(): pl.pallas_call(lambda *refs: gather_kernel(nz, *refs), out_shape=(kv_type...]
    all_to_all x8 -> x0, starting transfers between devices: 36.3 us -> none  [the longest x4 20.1 us: one_step(): lax.all_to_all(value_part, 'key', split_axis=1, concat_axis=0, tiled=True)]
    dot_general x24 -> x0, matrix products: 32 us -> none  [the longest x4 13 us: one_step(): jnp.einsum('gjhd,gkhd->ghjk', grad_heads, value_heads, preferred_element_...]
    while x8 -> x0, other arithmetic: 21.4 us -> none
    while x88 -> x0, local copies, waits for them, and re-layouts: 17.5 us -> none
  transfers between devices with their start and end apart: 10 -> 0, of which waited for: 6 -> 0; matrix products, arithmetic and copies ran while one was open for 4% -> 0% of each run, Pallas kernels for 0% -> 0%
where the time goes in v1:
time: 88.4 us; the launch traced here: 87 us
  Pallas kernels  80.4 us (91%)
  local copies, waits for them, and re-layouts  5.94 us (7%)
    pallas_call x1, Pallas kernels, per_device(): pl.pallas_call(lambda *refs: gather_kernel(nz, *refs), out_shape=(kv_type...  36.6 us
    pallas_call x1, Pallas kernels, per_device(): pl.pallas_call(lambda *refs: scatter_kernel(nz, *refs), out_shape=(kind,...  26.6 us
    pallas_call x1, Pallas kernels, per_device(): pl.pallas_call(lambda *refs: tile_kernel(nz, *refs), out_shape=(kv_type,...  17.2 us
    unnamed x7, local copies, waits for them, and re-layouts  3.21 us

profile of v1, /device:TPU:1, one launch (start us, length us, event | category | flops | bytes accessed | tf_op | source)
XLA Modules:
  0.0 87.0 jit_solution(14712452014039475495)
XLA Ops:
  0.6 1.3 %reshape.14.refs_4_ = bf16[4,16,128]{2,1,0:T(8,128)(2,1)} reshape(bf16[4,2,1024]{2,1,0:T(2,128)(2,1)} %param.10) | data formatting | bytes 32768 | tf_op jit(solution)/shard_map/reshape | solution.py:384
  2.0 36.6 %gather.1 = (bf16[2,4,32,1024]{3,2,1,0:T(8,128)(2,1)}, bf16[2,4,32,512]{3,2,1,0:T(8,128)(2,1)}, bf16[4,8,2,4,16,128]{5,4,3,2,1,0:T(8,128)(2,1)}) custom-call(bf16[4,128,128]{2,1,0:T(8,128)(2,1)} %refs_0_.2, bf16[4,128,128]{2,1,0:T(8,128)(2,1)} %refs_1_.1, bf16[4,128,128]{2,1,0:T(8,128)(2,1)} %refs_2_.1, bf16[4,128,128]{2,1,0:T(8,128)(2,1)} %refs_3_.1, ...), custom_call_target="tpu_custom_call" | custom-call | tf_op jit(solution)/shard_map/gather/pallas_call | solution.py:368
  38.6 17.2 %tiles.1 = (bf16[2,4,32,1024]{3,2,1,0:T(8,128)(2,1)}, bf16[4,32,512]{2,1,0:T(8,128)(2,1)}, bf16[4,8,2,4,16,128]{5,4,3,2,1,0:T(8,128)(2,1)}) custom-call(s32[4]{0:T(128)} %refs_0_.3, bf16[2,4,32,1024]{3,2,1,0:T(8,128)(2,1)} %get-tuple-element.14.refs_1_, bf16[2,4,32,512]{3,2,1,0:T(8,128)(2,1)} %get-tuple-element.15.refs_2_, ...), custom_call_target="tpu_custom_call" | custom-call | tf_op jit(solution)/shard_map/tiles/pallas_call | solution.py:386
  55.8 26.6 %scatter.1 = (bf16[4,128,128]{2,1,0:T(8,128)(2,1)}, bf16[4,128,128]{2,1,0:T(8,128)(2,1)}, bf16[4,128,128]{2,1,0:T(8,128)(2,1)}, f32[4,16,128]{2,1,0:T(8,128)}) custom-call(bf16[2,4,32,1024]{3,2,1,0:T(8,128)(2,1)} %get-tuple-element.17.refs_0_, bf16[4,32,512]{2,1,0:T(8,128)(2,1)} %get-tuple-element.18.refs_1_, ...), custom_call_target="tpu_custom_call" | custom-call | tf_op jit(solution)/shard_map/scatter/pallas_call | solution.py:405
  82.4 1.4 %reshape.15 = f32[4,2,1024]{2,1,0:T(2,128)} reshape(f32[4,16,128]{2,1,0:T(8,128)} %get-tuple-element.23) | data formatting | bytes 65536 | tf_op jit(solution)/shard_map/reshape | solution.py:430
  83.8 0.0 copy-start.1
  83.8 1.6 %copy.13 = bf16[4,128,128]{2,1,0:T(8,128)(2,1)} copy(bf16[4,128,128]{2,1,0:T(8,128)(2,1)} %get-tuple-element.28) | data formatting | bytes 262144
  85.4 0.0 copy-done.1
  85.4 0.0 copy-start
  85.4 0.7 copy.14
  86.0 0.3 copy-done
  86.3 0.7 copy.15
Async XLA Ops:
  83.8 1.6 %copy-start.1 = (bf16[4,128,128]{2,1,0:T(8,128)(2,1)S(1)}, bf16[4,128,128]{2,1,0:T(8,128)(2,1)}, u32[]{:S(2)}) copy-start(bf16[4,128,128]{2,1,0:T(8,128)(2,1)} %get-tuple-element.29) | copy-start | bytes 393220
  85.4 1.0 %copy-start = (bf16[4,128,128]{2,1,0:T(8,128)(2,1)S(1)}, bf16[4,128,128]{2,1,0:T(8,128)(2,1)}, u32[]{:S(2)}) copy-start(bf16[4,128,128]{2,1,0:T(8,128)(2,1)} %get-tuple-element.30) | copy-start | bytes 393220

commit v2 on v0

v2 whole, which is shorter than its diff:
```python
import math

import jax
import jax.numpy as jnp
from jax import lax
from jax.experimental import pallas as pl
from jax.experimental.pallas import tpu as pltpu
from jax.sharding import PartitionSpec as P

MESH = pl.DeviceIdType.MESH
VM = pltpu.VMEM
BF = jnp.bfloat16
F32 = jnp.float32
NX, NA = 4, 2
NY, NC = 8, 2
LOG2E = 1.4426950408889634


def place():
    row, key = lax.axis_index("row"), lax.axis_index("key")
    return (
        row,
        key,
        lax.div(key, NX),
        lax.rem(key, NX),
        lax.div(row, NY * NC),
        lax.rem(lax.div(row, NC), NY),
        lax.rem(row, NC),
    )


def row_of(z, y, core):
    return (z * NY + y) * NC + core


def peers_of(nz):
    row, key, a, x, z, y, core = place()
    peers = [(row, lax.rem(key + s, NA * NX)) for s in range(1, NA * NX)]
    peers += [(row_of(lax.rem(z + s, nz), y, core), key) for s in range(1, nz)]
    peers += [(row_of(z, lax.rem(y + s, NY), core), key) for s in range(1, NY)]
    peers += [(row_of(z, y, 1 - core), key)]
    return peers


def remote(src, dst, sems, index, peer):
    return pltpu.make_async_remote_copy(
        src_ref=src,
        dst_ref=dst,
        send_sem=sems[0].at[index],
        recv_sem=sems[1].at[index],
        device_id=peer,
        device_id_type=MESH,
    )


def start(copies):
    for cp in copies:
        cp.start()
    return copies


def wait(copies):
    for cp in copies:
        cp.wait()


def kernel(
    nz, lengths, q, k, v, c, bias, oq, ok, ov, ob,
    pieces, own, bg, kvs, qcs, kv, qc, q3, k3, cs, stage, eb, e, gws, total, acc, dkv, gq,
    gbs, r1, s1, r2a, r2b, s2a, s2b, r3a, r3b, s3, r4, rk, rq, loc, *pairs,
):
    row, key, a, x, z, y, core = place()
    rows_dev, block, feature = q.shape
    length = bias.shape[2]
    dim = feature // NX
    factor = 1.0 / math.sqrt(dim)
    sems = [(pairs[n], pairs[n + 1]) for n in range(0, len(pairs), 2)]
    m0, m1a, m1b, m2, m3, mkv, mqc, n1, n2, n3, n4, nkv, ngq = sems
    partner = (row_of(z, y, 1 - core), key)

    def y_peer(s):
        return (row_of(z, lax.rem(y + s, NY), core), key)

    def z_peer(s):
        return (row_of(lax.rem(z + s, nz), y, core), key)

    def x_peer(s):
        return (row, a * NX + lax.rem(x + s, NX))

    barrier = pltpu.get_barrier_semaphore()
    peers = peers_of(nz)
    for peer in peers:
        pl.semaphore_signal(barrier, inc=1, device_id=peer, device_id_type=MESH)

    for h in range(NX):
        lines = bias[h].astype(F32)
        for j in range(2):
            for t in range(8):
                n = h * 16 + j * 8 + t
                stage[n : n + 1, :] = lines[j : j + 1, t * 128 : (t + 1) * 128]
    for h in range(NX):
        pieces[h] = stage[h * 16 : (h + 1) * 16, :].astype(BF)
    for held, sources in ((kvs, (k, v)), (qcs, (q, c))):
        for part, source in enumerate(sources):
            for i in range(rows_dev):
                turned = source[i].T
                for h in range(NX):
                    held[h, part, i] = turned[h * dim : (h + 1) * dim]
    own[x] = pieces[x]
    pl.semaphore_wait(barrier, len(peers))

    first = start(
        [remote(pieces.at[lax.rem(x + s, NX)], own.at[x], m0, s - 1, x_peer(s)) for s in range(1, NX)]
    )
    others = []
    for s in range(1, NA * NX):
        to = lax.rem(key + s, NA * NX)
        others.append(
            remote(
                kvs.at[lax.rem(to, NX)], kv.at[:, :, :, pl.ds(key * 128, 128)], mkv, s - 1, (row, to)
            )
        )
    for s in range(1, NX):
        to = lax.rem(x + s, NX)
        others.append(
            remote(qcs.at[to], qc.at[:, :, :, pl.ds(x * 128, 128)], mqc, s - 1, x_peer(s))
        )
    start(others)
    mine = start(
        [
            pltpu.make_async_copy(kvs.at[x], kv.at[:, :, :, pl.ds(key * 128, 128)], loc.at[0]),
            pltpu.make_async_copy(qcs.at[x], qc.at[:, :, :, pl.ds(x * 128, 128)], loc.at[1]),
        ]
    )
    wait(first)
    phase1a = start(
        [
            remote(own.at[0:2], bg.at[0:2, core, z, y], m1a, s - 1, z_peer(s))
            for s in range(1, nz)
        ]
    )
    phase1b = start(
        [
            remote(own.at[2:4], bg.at[2:4, core, z, y], m1b, s - 1, y_peer(s))
            for s in range(1, NY)
        ]
    )
    for b in range(NX):
        bg[b, core, z, y] = own[b]
    phase2 = {}

    def spread(b):
        if b < 2:
            piece = bg.at[b, core, :, y]
            phase2[b] = [remote(piece, piece, m2, b * 7 + s - 1, y_peer(s)) for s in range(1, NY)]
        else:
            piece = bg.at[b, core, z]
            phase2[b] = [remote(piece, piece, m2, b * 7 + s - 1, z_peer(s)) for s in range(1, nz)]
        start(phase2[b])

    wait(phase1a)
    spread(0)
    wait(phase1b)
    spread(2)
    spread(3)
    spread(1)

    wait(mine + others)
    lane = lax.broadcasted_iota(jnp.int32, (16, length), 1)
    line = lax.broadcasted_iota(jnp.int32, (16, length), 0)
    span = NX * block
    for i in range(rows_dev):
        scaled = qc[0, i].astype(F32) * (factor * LOG2E)
        hi = scaled.astype(BF)
        rest = scaled - hi.astype(F32)
        mid = rest.astype(BF)
        low = (rest - mid.astype(F32)).astype(BF)
        ones = jnp.where(lax.broadcasted_iota(jnp.int32, (dim, span), 0) == 0, 1.0, 0.0).astype(BF)
        q3[i] = jnp.concatenate([hi, mid, low, ones], axis=0).T
        cs[i] = qc[1, i].T
        for n in range(3):
            k3[i, n * dim : (n + 1) * dim] = kv[0, i]
        hidden = jnp.where((line == 0) & (lane >= lengths[i]), -1e30, 0.0).astype(BF)
        k3[i, 3 * dim : 3 * dim + 16] = hidden
        k3[i, 3 * dim + 16 :] = jnp.zeros((dim - 16, length), BF)

    def early(n, carry):
        i, half = n // 2, n % 2
        rows = pl.ds(pl.multiple_of(half * 256, 256), 256)
        s = jnp.dot(q3[i, rows], k3[i], preferred_element_type=F32)
        e[i, rows] = jnp.exp2(s - jnp.max(s, axis=1, keepdims=True))
        gws[i, rows] = jnp.dot(cs[i, rows], kv[1, i], preferred_element_type=F32)
        return carry

    lax.fori_loop(0, 2 * rows_dev, early, 0)
    acc[...] = jnp.zeros_like(acc)
    total[...] = jnp.zeros_like(total)

    swaps = {}

    def hand(b):
        wait(phase2[b])
        swaps[b] = start([remote(bg.at[b, core], bg.at[b, core], m3, b, partner)])

    def lay(b):
        def part(zz, carry):
            for g in range(NY * NC):
                stage[g * 16 : (g + 1) * 16, :] = bg[b, g % NC, zz, g // NC].astype(F32) * LOG2E
            for g in range(NY * NC // 4):
                for t in range(8):
                    j0 = pl.multiple_of(b * block + zz * (NY * NC * 2) + g * 8, 8)
                    eb[pl.ds(j0, 8), t * 128 : (t + 1) * 128] = jnp.exp2(
                        stage[pl.ds(g * 64 + t, 8, stride=8), :]
                    )
            return carry

        lax.fori_loop(0, nz, part, 0)

    def late(b):
        rows = slice(b * block, (b + 1) * block)

        def one(i, carry):
            p = e[i, rows] * eb[rows]
            gw = gws[i, rows]
            inv = 1.0 / jnp.sum(p, axis=1, keepdims=True)
            w = p * inv
            g = w * (gw - jnp.sum(p * gw, axis=1, keepdims=True) * inv)
            total[rows] += g
            gl = g.astype(BF)
            gq[i, :, rows] = (
                lax.dot_general(
                    kv[0, i], gl, (((1,), (1,)), ((), ())), preferred_element_type=F32
                )
                * factor
            ).astype(BF)
            acc[0, i] += jnp.dot(qc[0, i, :, rows], gl, preferred_element_type=F32)
            acc[1, i] += jnp.dot(qc[1, i, :, rows], w.astype(BF), preferred_element_type=F32)
            return carry

        lax.fori_loop(0, rows_dev, one, 0, unroll=2)

    def unlay(b):
        def part(zz, carry):
            for g in range(NY * NC // 4):
                for t in range(8):
                    j0 = pl.multiple_of(b * block + zz * (NY * NC * 2) + g * 8, 8)
                    stage[pl.ds(g * 64 + t, 8, stride=8), :] = total[
                        pl.ds(j0, 8), t * 128 : (t + 1) * 128
                    ]
            for g in range(NY * NC):
                gbs[b, g % NC, zz, g // NC] = stage[g * 16 : (g + 1) * 16, :].astype(BF)
            return carry

        lax.fori_loop(0, nz, part, 0)

    flying = {}

    def swap(b):
        flying[1, b] = start([remote(gbs.at[b, 1 - core], r1.at[b], n1, b, partner)])

    def join(b):
        wait(flying[1, b])
        s1[b] = (gbs[b, core].astype(F32) + r1[b].astype(F32)).astype(BF)
        if b < 2:
            copies = [
                remote(s1.at[b, :, lax.rem(y + s, NY)], r2a.at[b, s - 1], n2, b * 7 + s - 1, y_peer(s))
                for s in range(1, NY)
            ]
        else:
            copies = [
                remote(s1.at[b, lax.rem(z + s, nz)], r2b.at[b - 2, s - 1], n2, b * 7 + s - 1, z_peer(s))
                for s in range(1, nz)
            ]
        flying[2, b] = start(copies)

    def second(b):
        wait(flying[2, b])
        if b < 2:
            part = s1[b, :, y].astype(F32)
            for s in range(NY - 1):
                part += r2a[b, s].astype(F32)
            s2a[b] = part.astype(BF)
            copies = [
                remote(s2a.at[b, lax.rem(z + s, nz)], r3a.at[b, s - 1], n3, b * 7 + s - 1, z_peer(s))
                for s in range(1, nz)
            ]
        else:
            part = s1[b, z].astype(F32)
            for s in range(nz - 1):
                part += r2b[b - 2, s].astype(F32)
            s2b[b - 2] = part.astype(BF)
            copies = [
                remote(s2b.at[b - 2, lax.rem(y + s, NY)], r3b.at[b - 2, s - 1], n3, b * 7 + s - 1, y_peer(s))
                for s in range(1, NY)
            ]
        flying[3, b] = start(copies)

    def third(b):
        wait(flying[3, b])
        if b < 2:
            part = s2a[b, z].astype(F32)
            for s in range(nz - 1):
                part += r3a[b, s].astype(F32)
        else:
            part = s2b[b - 2, y].astype(F32)
            for s in range(NY - 1):
                part += r3b[b - 2, s].astype(F32)
        s3[b] = part

    order = (0, 2, 3, 1)
    hand(0)
    hand(2)
    for n, b in enumerate(order):
        if n == 1:
            hand(3)
        if n == 2:
            hand(1)
        wait(swaps[b])
        lay(b)
        late(b)
        unlay(b)
        swap(b)
        if n >= 1:
            join(order[n - 1])
        if n >= 2:
            second(order[n - 2])

    for i in range(rows_dev):
        dkv[0, i] = (acc[0, i] * factor).astype(BF)
        dkv[1, i] = acc[1, i].astype(BF)
    outs = []
    for s in range(1, NA * NX):
        to = lax.rem(key + s, NA * NX)
        outs.append(
            remote(dkv.at[:, :, :, pl.ds(to * 128, 128)], rk.at[key], nkv, s - 1, (row, to))
        )
    for s in range(1, NX):
        to = lax.rem(x + s, NX)
        outs.append(remote(gq.at[:, :, pl.ds(to * 128, 128)], rq.at[x], ngq, s - 1, x_peer(s)))
    start(outs)
    held = start(
        [
            pltpu.make_async_copy(dkv.at[:, :, :, pl.ds(key * 128, 128)], rk.at[key], loc.at[2]),
            pltpu.make_async_copy(gq.at[:, :, pl.ds(x * 128, 128)], rq.at[x], loc.at[3]),
        ]
    )
    join(order[3])
    second(order[2])
    third(order[0])
    second(order[3])
    third(order[1])
    third(order[2])
    third(order[3])
    last = start(
        [
            remote(s3.at[lax.rem(x + s, NX)], r4.at[x], n4, s - 1, x_peer(s))
            for s in range(1, NX)
        ]
    )
    r4[x] = s3[x]
    wait(held + outs)
    for i in range(rows_dev):
        oq[i] = jnp.concatenate([rq[h, i] for h in range(NX)], axis=0).T
        for part, out in enumerate((ok, ov)):
            both = [
                rk[h, part, i].astype(F32) + rk[NX + h, part, i].astype(F32) for h in range(NX)
            ]
            out[i] = jnp.concatenate(both, axis=0).astype(BF).T
    wait(last)
    for h in range(NX):
        for j in range(2):
            for t in range(8):
                n = j * 8 + t
                ob[h, j : j + 1, t * 128 : (t + 1) * 128] = r4[h, n : n + 1, :]


def dma(*shape):
    return pltpu.SemaphoreType.DMA(shape)


def per_device(queries, keys_in, values, cotangent, pair_bias, key_lengths):
    rows_dev, block, feature = queries.shape
    heads, owned, length = pair_bias.shape
    dim = feature // heads
    nz = lax.axis_size("row") // (NY * NC)
    tile = (owned * length // 128, 128)
    span = NX * block
    vmem = pl.BlockSpec(memory_space=VM)
    kind = jax.ShapeDtypeStruct(queries.shape, BF)
    scratch = [
        VM((NX,) + tile, BF),
        VM((NX,) + tile, BF),
        VM((NX, NC, nz, NY) + tile, BF),
        VM((NX, 2, rows_dev, dim, block), BF),
        VM((NX, 2, rows_dev, dim, block), BF),
        VM((2, rows_dev, dim, length), BF),
        VM((2, rows_dev, dim, span), BF),
        VM((rows_dev, span, 4 * dim), BF),
        VM((rows_dev, 4 * dim, length), BF),
        VM((rows_dev, span, dim), BF),
        VM((NY * NC * tile[0], 128), F32),
        VM((span, length), F32),
        VM((rows_dev, span, length), F32),
        VM((rows_dev, span, length), F32),
        VM((span, length), F32),
        VM((2, rows_dev, dim, length), F32),
        VM((2, rows_dev, dim, length), BF),
        VM((rows_dev, dim, span), BF),
        VM((NX, NC, nz, NY) + tile, BF),
        VM((NX, nz, NY) + tile, BF),
        VM((NX, nz, NY) + tile, BF),
        VM((2, NY - 1, nz) + tile, BF),
        VM((2, nz - 1, NY) + tile, BF),
        VM((2, nz) + tile, BF),
        VM((2, NY) + tile, BF),
        VM((2, nz - 1) + tile, BF),
        VM((2, NY - 1) + tile, BF),
        VM((NX,) + tile, F32),
        VM((NX,) + tile, F32),
        VM((NA * NX, 2, rows_dev, dim, block), BF),
        VM((NX, rows_dev, dim, block), BF),
        dma(4),
    ]
    counts = (NX - 1, nz - 1, NY - 1, 28, NX, NA * NX - 1, NX - 1)
    counts += (NX, 28, 28, NX - 1, NA * NX - 1, NX - 1)
    scratch += [dma(n) for n in counts for _ in range(2)]
    return pl.pallas_call(
        lambda *refs: kernel(nz, *refs),
        out_shape=(kind, kind, kind, jax.ShapeDtypeStruct(pair_bias.shape, F32)),
        in_specs=[pl.BlockSpec(memory_space=pltpu.SMEM)] + [vmem] * 5,
        out_specs=(vmem,) * 4,
        scratch_shapes=scratch,
        compiler_params=pltpu.CompilerParams(
            collective_id=0, has_side_effects=True, vmem_limit_bytes=60 * 1024 * 1024
        ),
        name="attention_grad",
    )(key_lengths, queries, keys_in, values, cotangent, pair_bias)


def solution(mesh):
    wide = P("row", "key", None)
    bias = P(None, ("key", "row"), None)
    return jax.shard_map(
        per_device,
        mesh=mesh,
        in_specs=(wide, wide, wide, wide, bias, P("row")),
        out_specs=(wide, wide, wide, bias),
        check_vma=False,
    )
```

time: 1020 us -> 68.8 us (0.07)
  the two profiles are of different devices: /device:TPU:1 before, /device:TPU:4 now
where the time goes in v2:
time: 68.8 us; the launch traced here: 68.6 us
  Pallas kernels  64 us (93%)
  local copies, waits for them, and re-layouts  3.93 us (6%)
    pallas_call x1, Pallas kernels, per_device(): pl.pallas_call(lambda *refs: kernel(nz, *refs), out_shape=(kind, kind, ki...  64 us
    unnamed x10, local copies, waits for them, and re-layouts  3.93 us

profile of v2, /device:TPU:4, one launch (start us, length us, event | category | flops | bytes accessed | tf_op | source)
XLA Modules:
  0.0 68.6 jit_solution(16297931187186790129)
XLA Ops:
  0.6 64.0 %attention_grad.1 = (bf16[4,128,128]{2,1,0:T(8,128)(2,1)}, bf16[4,128,128]{2,1,0:T(8,128)(2,1)}, bf16[4,128,128]{2,1,0:T(8,128)(2,1)}, f32[4,2,1024]{2,1,0:T(2,128)}) custom-call(s32[4]{0:T(128)} %refs_0_.1, bf16[4,128,128]{2,1,0:T(8,128)(2,1)} %refs_1_.1, bf16[4,128,128]{2,1,0:T(8,128)(2,1)} %refs_2_.1, bf16[4,128,128]{2,1,0:T(8,128)(2,1)} %refs_3_.1, ...), custom_call_target="tpu_custom_call" | custom-call | tf_op jit(solution)/shard_map/attention_grad/pallas_call | solution.py:427
  64.6 0.0 copy-start.1
  64.7 1.6 %copy.14 = bf16[4,128,128]{2,1,0:T(8,128)(2,1)} copy(bf16[4,128,128]{2,1,0:T(8,128)(2,1)} %get-tuple-element.8) | data formatting | bytes 262144
  66.3 0.0 copy-done.1
  66.3 0.0 copy-start
  66.3 0.7 copy.15
  66.9 0.3 copy-done
  67.2 0.0 copy-start.2
  67.2 0.7 copy.16
  67.9 0.1 copy-done.2
  68.0 0.6 copy.17
Async XLA Ops:
  64.6 1.6 %copy-start.1 = (bf16[4,128,128]{2,1,0:T(8,128)(2,1)S(1)}, bf16[4,128,128]{2,1,0:T(8,128)(2,1)}, u32[]{:S(2)}) copy-start(bf16[4,128,128]{2,1,0:T(8,128)(2,1)} %get-tuple-element.9) | copy-start | bytes 393220
  66.3 1.0 %copy-start = (bf16[4,128,128]{2,1,0:T(8,128)(2,1)S(1)}, bf16[4,128,128]{2,1,0:T(8,128)(2,1)}, u32[]{:S(2)}) copy-start(bf16[4,128,128]{2,1,0:T(8,128)(2,1)} %get-tuple-element.10) | copy-start | bytes 393220
  67.2 0.8 %copy-start.2 = (f32[4,2,1024]{2,1,0:T(2,128)S(1)}, f32[4,2,1024]{2,1,0:T(2,128)}, u32[]{:S(2)}) copy-start(f32[4,2,1024]{2,1,0:T(2,128)} %get-tuple-element.11) | copy-start | bytes 98308

commit v3 on v2

v3 whole, which is shorter than its diff:
```python
import math

import jax
import jax.numpy as jnp
from jax import lax
from jax.experimental import pallas as pl
from jax.experimental.pallas import tpu as pltpu
from jax.sharding import PartitionSpec as P

MESH = pl.DeviceIdType.MESH
VM = pltpu.VMEM
BF = jnp.bfloat16
F32 = jnp.float32
NX, NA = 4, 2
NY, NC = 8, 2
LOG2E = 1.4426950408889634


def place():
    row, key = lax.axis_index("row"), lax.axis_index("key")
    return (
        row,
        key,
        lax.div(key, NX),
        lax.rem(key, NX),
        lax.div(row, NY * NC),
        lax.rem(lax.div(row, NC), NY),
        lax.rem(row, NC),
    )


def row_of(z, y, core):
    return (z * NY + y) * NC + core


def remote(src, dst, sems, out, back, peer):
    return pltpu.make_async_remote_copy(
        src_ref=src,
        dst_ref=dst,
        send_sem=sems[0].at[out],
        recv_sem=sems[1].at[back],
        device_id=peer,
        device_id_type=MESH,
    )


def start(copies):
    for cp in copies:
        cp.start()
    return copies


def wait(copies):
    for cp in copies:
        cp.wait()


def far_first(n):
    return sorted(range(1, n), key=lambda s: -min(s, n - s))


def kernel(
    nz, lengths, q, k, v, c, bias, rq, ks, r4,
    pieces, own, bg, kvs, qcs, kv, qc, lens, stage, eb, e, gws, total, acc, dkv, gq, rd,
    sd, gbs, r2a, r2b, s2a, s2b, r3a, r3b, s3, rk, loc, *pairs,
):
    row, key, a, x, z, y, core = place()
    rows_dev, block, feature = q.shape
    length = bias.shape[2]
    dim = feature // NX
    factor = 1.0 / math.sqrt(dim)
    sems = [(pairs[n], pairs[n + 1]) for n in range(0, len(pairs), 2)]
    m0, m1a, m1b, m2a, m2b, mkv, mqc, mswap, n2a, n2b, n3a, n3b, n4, nkv, ngq, nswap, mlen = sems
    other = row_of(z, y, 1 - core)
    half = lax.div(x, 2)
    side = lax.rem(x, 2)
    here = half == core

    def y_peer(s):
        return (row_of(z, lax.rem(y + s, NY), core), key)

    def z_peer(s):
        return (row_of(lax.rem(z + s, nz), y, core), key)

    ys, zs, xs = far_first(NY), far_first(nz), far_first(NX)
    barrier = pltpu.get_barrier_semaphore()
    peers = [(row, lax.rem(key + s, NA * NX)) for s in range(1, NA * NX)]
    peers += [(other, a * NX + lax.rem(x + s, NX)) for s in range(NX)]
    peers += [z_peer(s) for s in zs] + [y_peer(s) for s in ys]
    for peer in peers:
        pl.semaphore_signal(barrier, inc=1, device_id=peer, device_id_type=MESH)

    for h in range(NX):
        lines = bias[h].astype(F32)
        for j in range(2):
            for t in range(8):
                n = h * 16 + j * 8 + t
                stage[n : n + 1, :] = lines[j : j + 1, t * 128 : (t + 1) * 128]
    for h in range(NX):
        pieces[h] = stage[h * 16 : (h + 1) * 16, :].astype(BF)
    for held, sources in ((kvs, (k, v)), (qcs, (q, c))):
        for part, source in enumerate(sources):
            for i in range(rows_dev):
                turned = source[i].T
                for h in range(NX):
                    held[h, part, i] = turned[h * dim : (h + 1) * dim]
    spots = lax.broadcasted_iota(jnp.int32, (8, 128), 0)
    known = jnp.zeros((8, 128), F32)
    for i in range(rows_dev):
        known = jnp.where(spots == i, lengths[i].astype(F32), known)
    lens[core] = known
    pl.semaphore_wait(barrier, len(peers))

    target = row_of(z, y, half)

    def heads(source, dest, sems):
        return [
            remote(
                source.at[lax.rem(x + s, NX)], dest, sems, s, side * NC + core,
                (target, a * NX + lax.rem(x + s, NX)),
            )
            for s in [2, 1, 3, 0]
        ]

    def arrivals(source, dest, sems):
        for b in range(2):
            for g in range(NC):
                mine = (x == core * 2 + b) & (core == g)

                @pl.when(jnp.logical_not(mine))
                def _():
                    remote(
                        source.at[0], dest(b, g), sems, 0, b * NC + g, (other, key)
                    ).wait_recv()

    def launch(copies):
        start(copies[:-1])
        pl.when(jnp.logical_not(here))(copies[-1].start)

    def sent(copies):
        for cp in copies[:-1]:
            cp.wait_send()
        pl.when(jnp.logical_not(here))(copies[-1].wait_send)

    first = heads(pieces, own.at[side, core], m0)
    launch(first)

    @pl.when(here)
    def _():
        own[side, core] = pieces[x]

    tell = start([remote(lens.at[core], lens.at[core], mlen, 0, 0, (other, key))])
    others = []
    for s in (6, 2, 5, 7, 1, 3, 4):
        to = lax.rem(key + s, NA * NX)
        others.append(
            remote(
                kvs.at[lax.rem(to, NX)], kv.at[core, :, :, :, pl.ds(key * 128, 128)],
                mkv, s - 1, s - 1, (row, to),
            )
        )
    start(others)
    mine = start(
        [pltpu.make_async_copy(kvs.at[x], kv.at[core, :, :, :, pl.ds(key * 128, 128)], loc.at[0])]
    )

    def qc_place(b, g):
        return qc.at[g, :, :, :, b * 128 : (b + 1) * 128]

    asks = heads(qcs, qc.at[core, :, :, :, pl.ds(side * 128, 128)], mqc)
    launch(asks)
    keep = pltpu.make_async_copy(
        qcs.at[x], qc.at[core, :, :, :, pl.ds(side * 128, 128)], loc.at[1]
    )
    pl.when(here)(keep.start)

    arrivals(pieces, lambda b, g: own.at[b, g], m0)
    phase1a = start([remote(own.at[0], bg.at[0, z, y], m1a, s - 1, s - 1, z_peer(s)) for s in zs])
    phase1b = start([remote(own.at[1], bg.at[1, z, y], m1b, s - 1, s - 1, y_peer(s)) for s in ys])
    for b in range(2):
        bg[b, z, y] = own[b]
    wait(phase1a)
    piece = bg.at[0, :, y]
    phase2a = start([remote(piece, piece, m2a, s - 1, s - 1, y_peer(s)) for s in ys])
    wait(phase1b)
    piece = bg.at[1, z]
    phase2b = start([remote(piece, piece, m2b, s - 1, s - 1, z_peer(s)) for s in zs])

    wait(mine + others)
    swap = start([remote(kv.at[core], kv.at[core], mswap, 0, 0, (other, key))])
    arrivals(qcs, qc_place, mqc)
    pl.when(here)(keep.wait)
    lane = lax.broadcasted_iota(jnp.int32, (16, length), 1).astype(F32)
    line = lax.broadcasted_iota(jnp.int32, (16, length), 0)
    span = 2 * block

    def early(n, carry):
        g, i = n // rows_dev, n % rows_dev
        scaled = qc[g, 0, i].astype(F32) * (factor * LOG2E)
        hi = scaled.astype(BF)
        rest = scaled - hi.astype(F32)
        mid = rest.astype(BF)
        low = (rest - mid.astype(F32)).astype(BF)
        ones = jnp.where(lax.broadcasted_iota(jnp.int32, (dim, span), 0) == 0, 1.0, 0.0).astype(BF)
        q3 = jnp.concatenate([hi, mid, low, ones], axis=0).T
        keys = kv[g, 0, i]
        valid = jnp.concatenate([lens[g, pl.ds(i, 1), :]] * (length // 128), axis=1)
        hidden = jnp.where((line == 0) & (lane >= valid), -1e30, 0.0).astype(BF)
        k3 = jnp.concatenate([keys, keys, keys, hidden, jnp.zeros_like(hidden)], axis=0)
        s = jnp.dot(q3, k3, preferred_element_type=F32)
        e[g, i] = jnp.exp2(s - jnp.max(s, axis=1, keepdims=True))
        gws[g, i] = jnp.dot(qc[g, 1, i].T, kv[g, 1, i], preferred_element_type=F32)
        return carry

    def early_rows(g):
        lax.fori_loop(g * rows_dev, (g + 1) * rows_dev, early, 0)

    early_rows(core)
    wait(swap + tell)
    early_rows(1 - core)
    acc[...] = jnp.zeros_like(acc)
    total[...] = jnp.zeros_like(total)

    def lay(b):
        def part(zz, carry):
            stage[...] = bg[b, zz].astype(F32).reshape(NY * NC * 16, 128) * LOG2E
            for g in range(NY * NC // 4):
                for t in range(8):
                    j0 = pl.multiple_of(b * block + zz * (NY * NC * 2) + g * 8, 8)
                    eb[pl.ds(j0, 8), t * 128 : (t + 1) * 128] = jnp.exp2(
                        stage[pl.ds(g * 64 + t, 8, stride=8), :]
                    )
            return carry

        lax.fori_loop(0, nz, part, 0)

    def late(b, g):
        rows = slice(b * block, (b + 1) * block)

        def one(i, carry):
            p = e[g, i, rows] * eb[rows]
            gw = gws[g, i, rows]
            inv = 1.0 / jnp.sum(p, axis=1, keepdims=True)
            w = p * inv
            grad = w * (gw - jnp.sum(p * gw, axis=1, keepdims=True) * inv)
            total[rows] += grad
            low = grad.astype(BF)
            gq[g, i, :, rows] = (
                lax.dot_general(
                    kv[g, 0, i], low, (((1,), (1,)), ((), ())), preferred_element_type=F32
                )
                * factor
            ).astype(BF)
            acc[g, 0, i] += jnp.dot(qc[g, 0, i, :, rows], low, preferred_element_type=F32)
            acc[g, 1, i] += jnp.dot(
                qc[g, 1, i, :, rows], w.astype(BF), preferred_element_type=F32
            )
            return carry

        lax.fori_loop(0, rows_dev, one, 0, unroll=2)

    def unlay(b):
        def part(zz, carry):
            for g in range(NY * NC // 4):
                for t in range(8):
                    j0 = pl.multiple_of(b * block + zz * (NY * NC * 2) + g * 8, 8)
                    stage[pl.ds(g * 64 + t, 8, stride=8), :] = total[
                        pl.ds(j0, 8), t * 128 : (t + 1) * 128
                    ]
            gbs[b, zz] = stage[...].reshape(NY, NC, 16, 128).astype(BF)
            return carry

        lax.fori_loop(0, nz, part, 0)

    wait(phase2a)
    lay(0)
    late(0, 1 - core)
    late(0, core)
    unlay(0)
    sum2a = start(
        [
            remote(gbs.at[0, :, lax.rem(y + s, NY)], r2a.at[s - 1], n2a, s - 1, s - 1, y_peer(s))
            for s in ys
        ]
    )
    wait(phase2b)
    lay(1)
    late(1, 1 - core)
    for i in range(rows_dev):
        dkv[1 - core, 0, i] = (acc[1 - core, 0, i] * factor).astype(BF)
        dkv[1 - core, 1, i] = acc[1 - core, 1, i].astype(BF)
    give = start([remote(dkv.at[1 - core], rd, nswap, 0, 0, (other, key))])
    late(1, core)
    unlay(1)
    sum2b = start(
        [
            remote(gbs.at[1, lax.rem(z + s, nz)], r2b.at[s - 1], n2b, s - 1, s - 1, z_peer(s))
            for s in zs
        ]
    )

    backs = []
    for b in range(2):
        for g in range(NC):
            away = jnp.logical_not((x == core * 2 + b) & (core == g))
            piece = gq.at[g, :, :, b * 128 : (b + 1) * 128]
            owner = (row_of(z, y, g), a * NX + core * 2 + b)
            cp = remote(piece, rq.at[x], ngq, b * NC + g, x, owner)
            pl.when(away)(cp.start)
            keep = pltpu.make_async_copy(piece, rq.at[x], loc.at[2])
            pl.when(jnp.logical_not(away))(keep.start)
            backs.append((away, cp, keep))
    wait(give)
    for i in range(rows_dev):
        sd[0, i] = (acc[core, 0, i] * factor + rd[0, i].astype(F32)).astype(BF)
        sd[1, i] = (acc[core, 1, i] + rd[1, i].astype(F32)).astype(BF)
    outs = []
    for s in (6, 2, 5, 7, 1, 3, 4):
        to = lax.rem(key + s, NA * NX)
        outs.append(
            remote(
                sd.at[:, :, :, pl.ds(to * 128, 128)], rk.at[key], nkv, s - 1, s - 1, (row, to)
            )
        )
    start(outs)
    held = start(
        [pltpu.make_async_copy(sd.at[:, :, :, pl.ds(key * 128, 128)], rk.at[key], loc.at[3])]
    )

    wait(sum2a)
    part = gbs[0, :, y].astype(F32)
    for s in range(NY - 1):
        part += r2a[s].astype(F32)
    s2a[...] = part.astype(BF)
    sum3a = start(
        [
            remote(s2a.at[lax.rem(z + s, nz)], r3a.at[s - 1], n3a, s - 1, s - 1, z_peer(s))
            for s in zs
        ]
    )
    wait(sum2b)
    part = gbs[1, z].astype(F32)
    for s in range(nz - 1):
        part += r2b[s].astype(F32)
    s2b[...] = part.astype(BF)
    sum3b = start(
        [
            remote(s2b.at[lax.rem(y + s, NY)], r3b.at[s - 1], n3b, s - 1, s - 1, y_peer(s))
            for s in ys
        ]
    )
    wait(sum3a)
    part = s2a[z].astype(F32)
    for s in range(nz - 1):
        part += r3a[s].astype(F32)
    s3[0] = part
    wait(sum3b)
    part = s2b[y].astype(F32)
    for s in range(NY - 1):
        part += r3b[s].astype(F32)
    s3[1] = part
    ends = []
    for b in range(2):
        for g in range(NC):
            away = jnp.logical_not((x == core * 2 + b) & (core == g))
            owner = (row_of(z, y, g), a * NX + core * 2 + b)
            cp = remote(s3.at[b, g], r4.at[x], n4, b * NC + g, x, owner)
            pl.when(away)(cp.start)
            ends.append((away, cp))

    @pl.when(here)
    def _():
        r4[x] = s3[side, core]

    wait(held + outs)
    for i in range(rows_dev):
        for part in range(2):
            for h in range(NX):
                ks[part, i, h * dim : (h + 1) * dim] = (
                    rk[h, part, i].astype(F32) + rk[NX + h, part, i].astype(F32)
                ).astype(BF)
    for away, cp, keep in backs:
        pl.when(away)(cp.wait_send)
        pl.when(jnp.logical_not(away))(keep.wait)
    for away, cp in ends:
        pl.when(away)(cp.wait_send)
    sent(first)
    sent(asks)
    for h in range(NX):

        @pl.when(jnp.logical_not((x == h) & here))
        def _():
            remote(gq.at[0, :, :, 0:128], rq.at[h], ngq, 0, h, (other, key)).wait_recv()
            remote(s3.at[0, 0], r4.at[h], n4, 0, h, (other, key)).wait_recv()


def finish(rq, ks, r4, oq, ok, ov, ob):
    for i in range(oq.shape[0]):
        oq[i] = jnp.concatenate([rq[h, i] for h in range(NX)], axis=0).T
        ok[i] = ks[0, i].T
        ov[i] = ks[1, i].T
    for h in range(NX):
        for j in range(2):
            for t in range(8):
                n = j * 8 + t
                ob[h, j : j + 1, t * 128 : (t + 1) * 128] = r4[h, n : n + 1, :]


def dma(*shape):
    return pltpu.SemaphoreType.DMA(shape)


def per_device(queries, keys_in, values, cotangent, pair_bias, key_lengths):
    rows_dev, block, feature = queries.shape
    heads, owned, length = pair_bias.shape
    dim = feature // heads
    nz = lax.axis_size("row") // (NY * NC)
    tile = (owned * length // 128, 128)
    span = 2 * block
    vmem = pl.BlockSpec(memory_space=VM)
    kind = jax.ShapeDtypeStruct(queries.shape, BF)
    scratch = [
        VM((NX,) + tile, BF),
        VM((2, NC) + tile, BF),
        VM((2, nz, NY, NC) + tile, BF),
        VM((NX, 2, rows_dev, dim, block), BF),
        VM((NX, 2, rows_dev, dim, block), BF),
        VM((NC, 2, rows_dev, dim, length), BF),
        VM((NC, 2, rows_dev, dim, span), BF),
        VM((NC, 8, 128), F32),
        VM((NY * NC * tile[0], 128), F32),
        VM((span, length), F32),
        VM((NC, rows_dev, span, length), F32),
        VM((NC, rows_dev, span, length), F32),
        VM((span, length), F32),
        VM((NC, 2, rows_dev, dim, length), F32),
        VM((NC, 2, rows_dev, dim, length), BF),
        VM((NC, rows_dev, dim, span), BF),
        VM((2, rows_dev, dim, length), BF),
        VM((2, rows_dev, dim, length), BF),
        VM((2, nz, NY, NC) + tile, BF),
        VM((NY - 1, nz, NC) + tile, BF),
        VM((nz - 1, NY, NC) + tile, BF),
        VM((nz, NC) + tile, BF),
        VM((NY, NC) + tile, BF),
        VM((nz - 1, NC) + tile, BF),
        VM((NY - 1, NC) + tile, BF),
        VM((2, NC) + tile, F32),
        VM((NA * NX, 2, rows_dev, dim, block), BF),
        dma(4),
    ]
    counts = (4, nz - 1, NY - 1, NY - 1, nz - 1, NA * NX - 1, 4, 1)
    counts += (NY - 1, nz - 1, nz - 1, NY - 1, 4, NA * NX - 1, 4, 1, 1)
    scratch += [dma(n) for n in counts for _ in range(2)]
    passed = (
        jax.ShapeDtypeStruct((NX, rows_dev, dim, block), BF),
        jax.ShapeDtypeStruct((2, rows_dev, feature, block), BF),
        jax.ShapeDtypeStruct((heads,) + tile, F32),
    )
    parts = pl.pallas_call(
        lambda *refs: kernel(nz, *refs),
        out_shape=passed,
        in_specs=[pl.BlockSpec(memory_space=pltpu.SMEM)] + [vmem] * 5,
        out_specs=(vmem,) * 3,
        scratch_shapes=scratch,
        compiler_params=pltpu.CompilerParams(
            collective_id=0, has_side_effects=True, vmem_limit_bytes=60 * 1024 * 1024
        ),
        name="attention_grad",
    )(key_lengths, queries, keys_in, values, cotangent, pair_bias)
    return pl.pallas_call(
        finish,
        out_shape=(kind, kind, kind, jax.ShapeDtypeStruct(pair_bias.shape, F32)),
        in_specs=[vmem] * 3,
        out_specs=(vmem,) * 4,
        compiler_params=pltpu.CompilerParams(vmem_limit_bytes=60 * 1024 * 1024),
        name="finish",
    )(*parts)


def solution(mesh):
    wide = P("row", "key", None)
    bias = P(None, ("key", "row"), None)
    return jax.shard_map(
        per_device,
        mesh=mesh,
        in_specs=(wide, wide, wide, wide, bias, P("row")),
        out_specs=(wide, wide, wide, bias),
        check_vma=False,
    )
```

time: 68.8 us -> 61.9 us (0.90)
  the two profiles are of different devices: /device:TPU:4 before, /device:TPU:1 now
where the time goes in v3:
time: 61.9 us; the launch traced here: 61.7 us
  Pallas kernels  61.1 us (99%)
  between operations  0.64 us (1%)
    pallas_call x1, Pallas kernels, per_device(): pl.pallas_call(lambda *refs: kernel(nz, *refs), out_shape=passed, in_spec...  59.2 us
    pallas_call x1, Pallas kernels, per_device(): pl.pallas_call(finish, out_shape=(kind, kind, kind, jax.ShapeDtypeStruct(...  1.87 us

profile of v3, /device:TPU:1, one launch (start us, length us, event | category | flops | bytes accessed | tf_op | source)
XLA Modules:
  0.0 61.7 jit_solution(9698219760056079252)
XLA Ops:
  0.6 59.2 %attention_grad.1 = (bf16[4,4,32,128]{3,2,1,0:T(8,128)(2,1)}, bf16[2,4,128,128]{3,2,1,0:T(8,128)(2,1)}, f32[4,16,128]{2,1,0:T(8,128)}) custom-call(s32[4]{0:T(128)} %refs_0_.1, bf16[4,128,128]{2,1,0:T(8,128)(2,1)} %refs_1_.1, bf16[4,128,128]{2,1,0:T(8,128)(2,1)} %refs_2_.1, bf16[4,128,128]{2,1,0:T(8,128)(2,1)} %refs_3_.1, bf16[4,128,128]{2,1,0:T(8,128)(2,1)} %refs_4_.1, ...), custom_call_target="tpu_custom_call" | custom-call | tf_op jit(solution)/shard_map/attention_grad/pallas_call | solution.py:460
  59.9 1.9 %finish.1 = (bf16[4,128,128]{2,1,0:T(8,128)(2,1)}, bf16[4,128,128]{2,1,0:T(8,128)(2,1)}, bf16[4,128,128]{2,1,0:T(8,128)(2,1)}, f32[4,2,1024]{2,1,0:T(2,128)}) custom-call(bf16[4,4,32,128]{3,2,1,0:T(8,128)(2,1)} %get-tuple-element.7.rq, bf16[2,4,128,128]{3,2,1,0:T(8,128)(2,1)} %get-tuple-element.8.ks, f32[4,16,128]{2,1,0:T(8,128)} %get-tuple-element.9.r4), custom_call_target="tpu_custom_call" | custom-call | tf_op jit(solution)/shard_map/finish/pallas_call | solution.py:471

commit v4 on v3

v4 whole, which is shorter than its diff:
```python
import math

import jax
import jax.numpy as jnp
from jax import lax
from jax.experimental import pallas as pl
from jax.experimental.pallas import tpu as pltpu
from jax.sharding import PartitionSpec as P

MESH = pl.DeviceIdType.MESH
VM = pltpu.VMEM
BF = jnp.bfloat16
F32 = jnp.float32
NX, NA = 4, 2
NY, NC = 8, 2
LOG2E = 1.4426950408889634
EXCHANGES = 21


def place():
    row, key = lax.axis_index("row"), lax.axis_index("key")
    return (
        row,
        key,
        lax.div(key, NX),
        lax.rem(key, NX),
        lax.div(row, NY * NC),
        lax.rem(lax.div(row, NC), NY),
        lax.rem(row, NC),
    )


def row_of(z, y, core):
    return (z * NY + y) * NC + core


def remote(src, dst, sems, peer):
    return pltpu.make_async_remote_copy(
        src_ref=src,
        dst_ref=dst,
        send_sem=sems[0],
        recv_sem=sems[1],
        device_id=peer,
        device_id_type=MESH,
    )


def take(sem, like):
    pltpu.make_async_copy(like, like, sem).wait()


def start(copies):
    for cp in copies:
        cp.start()
    return copies


def far_first(n):
    return sorted(range(1, n), key=lambda s: -min(s, n - s))


def kernel(
    nz, lengths, q, k, v, c, bias, rq, ks, r4,
    pieces, own, bg, kvs, qcs, kv, qc, qs, lens, stage, eb, e, gws, total, acc, dkv, gqs, gq, rd,
    sd, gbs, r2a, r2b, s2a, s2b, r3a, r3b, s3, rk, loc, out_sems, in_sems,
):
    row, key, a, x, z, y, core = place()
    rows_dev, block, feature = q.shape
    length = bias.shape[2]
    dim = feature // NX
    factor = 1.0 / math.sqrt(dim)
    sems = [(out_sems.at[n], in_sems.at[n]) for n in range(EXCHANGES)]
    m0, m1a, m1b, mkv, mqc, mswap, n3a, n3b, n4, nkv, ngq, nswap, mlen = sems[:13]
    m2, n2 = sems[13:17], sems[17:21]
    other = row_of(z, y, 1 - core)
    half = lax.div(x, 2)
    side = lax.rem(x, 2)
    here = half == core

    def y_peer(s):
        return (row_of(z, lax.rem(y + s, NY), core), key)

    def z_peer(s):
        return (row_of(lax.rem(z + s, nz), y, core), key)

    ys, zs, xs = far_first(NY), far_first(nz), far_first(NX)
    barrier = pltpu.get_barrier_semaphore()
    peers = [(row, lax.rem(key + s, NA * NX)) for s in range(1, NA * NX)]
    peers += [(other, a * NX + lax.rem(x + s, NX)) for s in range(NX)]
    peers += [z_peer(s) for s in zs] + [y_peer(s) for s in ys]
    for peer in peers:
        pl.semaphore_signal(barrier, inc=1, device_id=peer, device_id_type=MESH)

    for h in range(NX):
        lines = bias[h].astype(F32)
        for j in range(2):
            for t in range(8):
                n = h * 16 + j * 8 + t
                stage[n : n + 1, :] = lines[j : j + 1, t * 128 : (t + 1) * 128]
    for h in range(NX):
        pieces[h] = stage[h * 16 : (h + 1) * 16, :].astype(BF)
    spots = lax.broadcasted_iota(jnp.int32, (8, 128), 0)
    known = jnp.zeros((8, 128), F32)
    for i in range(rows_dev):
        known = jnp.where(spots == i, lengths[i].astype(F32), known)
    lens[core] = known
    pl.semaphore_wait(barrier, len(peers))

    target = row_of(z, y, half)

    def heads(source, dest, sems):
        return [
            remote(
                source.at[lax.rem(x + s, NX)], dest, sems, (target, a * NX + lax.rem(x + s, NX))
            )
            for s in [2, 1, 3, 0]
        ]

    def take_some(sem, like):
        pl.when(here)(lambda: take(sem, like.at[0:3]))
        pl.when(jnp.logical_not(here))(lambda: take(sem, like))

    def launch(copies):
        start(copies[:-1])
        pl.when(jnp.logical_not(here))(copies[-1].start)

    first = heads(pieces, own.at[side, core], m0)
    launch(first)

    @pl.when(here)
    def _():
        own[side, core] = pieces[x]

    tell = start([remote(lens.at[core], lens.at[core], mlen, (other, key))])
    for part, source in enumerate((k, v)):
        for i in range(rows_dev):
            turned = source[i].T
            for h in range(NX):
                kvs[h, part, i] = turned[h * dim : (h + 1) * dim]
    others = []
    for s in (6, 2, 5, 7, 1, 3, 4):
        to = lax.rem(key + s, NA * NX)
        others.append(
            remote(
                kvs.at[lax.rem(to, NX)], kv.at[core, :, :, :, pl.ds(key * 128, 128)],
                mkv, (row, to),
            )
        )
    start(others)
    mine = start(
        [pltpu.make_async_copy(kvs.at[x], kv.at[core, :, :, :, pl.ds(key * 128, 128)], loc.at[0])]
    )

    for part, source in enumerate((q, c)):
        for i in range(rows_dev):
            lines = []
            for n in range(2 * nz):
                at = jnp.where(side == 1, (n % nz) * 2 + n // nz, n)
                lines.append(source[i, pl.ds(pl.multiple_of(at * 16, 16), 16)])
            turned = jnp.concatenate(lines, axis=0).T
            for h in range(NX):
                qcs[h, part, i] = turned[h * dim : (h + 1) * dim]

    asks = heads(qcs, qc.at[core, :, :, :, pl.ds(side * 128, 128)], mqc)
    launch(asks)
    keep = pltpu.make_async_copy(
        qcs.at[x], qc.at[core, :, :, :, pl.ds(side * 128, 128)], loc.at[1]
    )
    pl.when(here)(keep.start)

    take_some(m0[1], pieces)
    phase1a = start([remote(own.at[0], bg.at[0, z, y], m1a, z_peer(s)) for s in zs])
    phase1b = start([remote(own.at[1], bg.at[1, z, y], m1b, y_peer(s)) for s in ys])
    for b in range(2):
        bg[b, z, y] = own[b]
    phase2 = {}
    take(m1a[1], r3a)
    for n in range(2):
        piece = bg.at[0, n * nz // 2 : (n + 1) * nz // 2, y]
        phase2[n] = start(
            [remote(piece, piece, m2[n], y_peer(s)) for s in ys]
        )
    take(m1b[1], r3b)
    for n in range(2):
        piece = bg.at[1, z, n * NY // 2 : (n + 1) * NY // 2]
        phase2[2 + n] = start(
            [remote(piece, piece, m2[2 + n], z_peer(s)) for s in zs]
        )

    take(mkv[1], rk.at[0:7])
    mine[0].wait()
    swap = start([remote(kv.at[core], kv.at[core], mswap, (other, key))])
    take_some(mqc[1], qcs)
    pl.when(here)(keep.wait)
    lane = lax.broadcasted_iota(jnp.int32, (16, length), 1).astype(F32)
    line = lax.broadcasted_iota(jnp.int32, (16, length), 0)
    span = 2 * block
    part_rows = span // 4

    def early(n, carry):
        g, i = n // rows_dev, n % rows_dev
        scaled = qc[g, 0, i].astype(F32) * (factor * LOG2E)
        hi = scaled.astype(BF)
        rest = scaled - hi.astype(F32)
        mid = rest.astype(BF)
        low = (rest - mid.astype(F32)).astype(BF)
        ones = jnp.where(lax.broadcasted_iota(jnp.int32, (dim, span), 0) == 0, 1.0, 0.0).astype(BF)
        q3 = jnp.concatenate([hi, mid, low, ones], axis=0).T
        keys = kv[g, 0, i]
        valid = jnp.concatenate([lens[g, pl.ds(i, 1), :]] * (length // 128), axis=1)
        hidden = jnp.where((line == 0) & (lane >= valid), -1e30, 0.0).astype(BF)
        k3 = jnp.concatenate([keys, keys, keys, hidden, jnp.zeros_like(hidden)], axis=0)
        s = jnp.dot(q3, k3, preferred_element_type=F32)
        e[g, i] = jnp.exp2(s - jnp.max(s, axis=1, keepdims=True))
        for part in range(2):
            lines = qc[g, part, i].T
            for n in range(4):
                qs[n, g, part, i] = lines[n * part_rows : (n + 1) * part_rows].T
        gws[g, i] = jnp.dot(qc[g, 1, i].T, kv[g, 1, i], preferred_element_type=F32)
        return carry

    def early_rows(g):
        lax.fori_loop(g * rows_dev, (g + 1) * rows_dev, early, 0)

    early_rows(core)
    take(mswap[1], rd)
    take(mlen[1], lens.at[0])
    early_rows(1 - core)
    acc[...] = jnp.zeros_like(acc)
    total[...] = jnp.zeros_like(total)

    def chunks(n):
        if n < 2:
            return nz // 2, NY, lambda zz: (0, n * nz // 2 + zz, slice(None))
        return nz, NY // 2, lambda zz: (1, zz, slice((n - 2) * NY // 2, (n - 1) * NY // 2))

    def lay(n):
        count, wide, at = chunks(n)

        def part(zz, carry):
            stage[: wide * NC * 16] = (
                bg[at(zz)].astype(F32).reshape(wide * NC * 16, 128) * LOG2E
            )
            for g in range(wide * NC // 4):
                for t in range(8):
                    j0 = pl.multiple_of(n * part_rows + zz * (wide * NC * 2) + g * 8, 8)
                    eb[pl.ds(j0, 8), t * 128 : (t + 1) * 128] = jnp.exp2(
                        stage[pl.ds(g * 64 + t, 8, stride=8), :]
                    )
            return carry

        lax.fori_loop(0, count, part, 0)

    def late(n, g):
        rows = slice(n * part_rows, (n + 1) * part_rows)

        def one(i, carry):
            p = e[g, i, rows] * eb[rows]
            gw = gws[g, i, rows]
            inv = 1.0 / jnp.sum(p, axis=1, keepdims=True)
            w = p * inv
            grad = w * (gw - jnp.sum(p * gw, axis=1, keepdims=True) * inv)
            total[rows] += grad
            low = grad.astype(BF)
            gqs[n, g, i] = lax.dot_general(
                kv[g, 0, i], low, (((1,), (1,)), ((), ())), preferred_element_type=F32
            )
            acc[g, 0, i] += jnp.dot(qs[n, g, 0, i], low, preferred_element_type=F32)
            acc[g, 1, i] += jnp.dot(qs[n, g, 1, i], w.astype(BF), preferred_element_type=F32)
            return carry

        lax.fori_loop(0, rows_dev, one, 0, unroll=4)

    def unlay(n):
        count, wide, at = chunks(n)

        def part(zz, carry):
            for g in range(wide * NC // 4):
                for t in range(8):
                    j0 = pl.multiple_of(n * part_rows + zz * (wide * NC * 2) + g * 8, 8)
                    stage[pl.ds(g * 64 + t, 8, stride=8), :] = total[
                        pl.ds(j0, 8), t * 128 : (t + 1) * 128
                    ]
            gbs[at(zz)] = stage[: wide * NC * 16].reshape(wide, NC, 16, 128).astype(BF)
            return carry

        lax.fori_loop(0, count, part, 0)

    order = (0, 2, 3, 1)
    sum2 = {}
    for turn, n in enumerate(order):
        take(m2[n][1], r2a.at[0] if n < 2 else r2b.at[0])
        lay(n)
        late(n, 1 - core)
        if turn == 3:
            for i in range(rows_dev):
                dkv[1 - core, 0, i] = (acc[1 - core, 0, i] * factor).astype(BF)
                dkv[1 - core, 1, i] = acc[1 - core, 1, i].astype(BF)
            give = start([remote(dkv.at[1 - core], rd, nswap, (other, key))])
        late(n, core)
        unlay(n)
        if n < 2:
            sum2[n] = [
                remote(
                    gbs.at[0, n * nz // 2 : (n + 1) * nz // 2, lax.rem(y + s, NY)],
                    r2a.at[n, s - 1], n2[n], y_peer(s),
                )
                for s in ys
            ]
        else:
            sum2[n] = [
                remote(
                    gbs.at[1, lax.rem(z + s, nz), (n - 2) * NY // 2 : (n - 1) * NY // 2],
                    r2b.at[n - 2, s - 1], n2[n], z_peer(s),
                )
                for s in zs
            ]
        start(sum2[n])
    for g in range(NC):
        for i in range(rows_dev):
            gq[g, i] = (
                jnp.concatenate([gqs[n, g, i] for n in range(4)], axis=1) * factor
            ).astype(BF)

    backs = []
    for b in range(2):
        for g in range(NC):
            away = jnp.logical_not((x == core * 2 + b) & (core == g))
            piece = gq.at[g, :, :, b * 128 : (b + 1) * 128]
            owner = (row_of(z, y, g), a * NX + core * 2 + b)
            cp = remote(piece, rq.at[x], ngq, owner)
            pl.when(away)(cp.start)
            keep = pltpu.make_async_copy(piece, rq.at[x], loc.at[2])
            pl.when(jnp.logical_not(away))(keep.start)
            backs.append((away, keep))
    take(nswap[1], rd)
    for i in range(rows_dev):
        sd[0, i] = (acc[core, 0, i] * factor + rd[0, i].astype(F32)).astype(BF)
        sd[1, i] = (acc[core, 1, i] + rd[1, i].astype(F32)).astype(BF)
    outs = []
    for s in (6, 2, 5, 7, 1, 3, 4):
        to = lax.rem(key + s, NA * NX)
        outs.append(
            remote(
                sd.at[:, :, :, pl.ds(to * 128, 128)], rk.at[key], nkv, (row, to)
            )
        )
    start(outs)
    held = start(
        [pltpu.make_async_copy(sd.at[:, :, :, pl.ds(key * 128, 128)], rk.at[key], loc.at[3])]
    )

    take(n2[2][1], r2b.at[0])
    take(n2[3][1], r2b.at[1])
    for n in range(2):
        part = gbs[1, z, n * NY // 2 : (n + 1) * NY // 2].astype(F32)
        for s in range(nz - 1):
            part += r2b[n, s].astype(F32)
        s2b[n * NY // 2 : (n + 1) * NY // 2] = part.astype(BF)
    sum3b = start(
        [
            remote(s2b.at[lax.rem(y + s, NY)], r3b.at[s - 1], n3b, y_peer(s))
            for s in ys
        ]
    )
    take(n2[0][1], r2a.at[0])
    take(n2[1][1], r2a.at[1])
    for n in range(2):
        part = gbs[0, n * nz // 2 : (n + 1) * nz // 2, y].astype(F32)
        for s in range(NY - 1):
            part += r2a[n, s].astype(F32)
        s2a[n * nz // 2 : (n + 1) * nz // 2] = part.astype(BF)
    sum3a = start(
        [
            remote(s2a.at[lax.rem(z + s, nz)], r3a.at[s - 1], n3a, z_peer(s))
            for s in zs
        ]
    )
    take(n3a[1], r3a)
    part = s2a[z].astype(F32)
    for s in range(nz - 1):
        part += r3a[s].astype(F32)
    s3[0] = part
    take(n3b[1], r3b)
    part = s2b[y].astype(F32)
    for s in range(NY - 1):
        part += r3b[s].astype(F32)
    s3[1] = part
    for b in range(2):
        for g in range(NC):
            away = jnp.logical_not((x == core * 2 + b) & (core == g))
            owner = (row_of(z, y, g), a * NX + core * 2 + b)
            cp = remote(s3.at[b, g], r4.at[x], n4, owner)
            pl.when(away)(cp.start)

    @pl.when(here)
    def _():
        r4[x] = s3[side, core]

    take(nkv[1], rk.at[0:7])
    held[0].wait()
    for i in range(rows_dev):
        for part in range(2):
            for h in range(NX):
                ks[part, i, h * dim : (h + 1) * dim] = (
                    rk[h, part, i].astype(F32) + rk[NX + h, part, i].astype(F32)
                ).astype(BF)
    for away, keep in backs:
        pl.when(jnp.logical_not(away))(keep.wait)
    take_some(ngq[1], rq)
    take_some(n4[1], r4)
    take_some(m0[0], pieces)
    take_some(mqc[0], qcs)
    take_some(ngq[0], rq)
    take_some(n4[0], r4)
    for group, like in (
        (m1a, r3a), (m1b, r3b), (n3a, r3a), (n3b, r3b), (mkv, rk.at[0:7]), (nkv, rk.at[0:7]),
        (mswap, rd), (nswap, rd), (mlen, lens.at[0]),
    ):
        take(group[0], like)
    for group in (m2, n2):
        for n in range(4):
            take(group[n][0], r2a.at[0] if n < 2 else r2b.at[0])


def finish(nz, rq, ks, r4, oq, ok, ov, ob, held):
    odd = lax.rem(lax.axis_index("key"), 2)
    for i in range(oq.shape[0]):
        held[...] = jnp.concatenate([rq[h, i] for h in range(NX)], axis=0).T
        for n in range(2 * nz):
            at = jnp.where(odd == 1, (n % 2) * nz + n // 2, n)
            oq[i, n * 16 : (n + 1) * 16] = held[pl.ds(pl.multiple_of(at * 16, 16), 16)]
        ok[i] = ks[0, i].T
        ov[i] = ks[1, i].T
    for h in range(NX):
        for j in range(2):
            for t in range(8):
                n = j * 8 + t
                ob[h, j : j + 1, t * 128 : (t + 1) * 128] = r4[h, n : n + 1, :]


def dma(*shape):
    return pltpu.SemaphoreType.DMA(shape)


def per_device(queries, keys_in, values, cotangent, pair_bias, key_lengths):
    rows_dev, block, feature = queries.shape
    heads, owned, length = pair_bias.shape
    dim = feature // heads
    nz = lax.axis_size("row") // (NY * NC)
    tile = (owned * length // 128, 128)
    span = 2 * block
    vmem = pl.BlockSpec(memory_space=VM)
    kind = jax.ShapeDtypeStruct(queries.shape, BF)
    scratch = [
        VM((NX,) + tile, BF),
        VM((2, NC) + tile, BF),
        VM((2, nz, NY, NC) + tile, BF),
        VM((NX, 2, rows_dev, dim, block), BF),
        VM((NX, 2, rows_dev, dim, block), BF),
        VM((NC, 2, rows_dev, dim, length), BF),
        VM((NC, 2, rows_dev, dim, span), BF),
        VM((4, NC, 2, rows_dev, dim, span // 4), BF),
        VM((NC, 8, 128), F32),
        VM((NY * NC * tile[0], 128), F32),
        VM((span, length), F32),
        VM((NC, rows_dev, span, length), F32),
        VM((NC, rows_dev, span, length), F32),
        VM((span, length), F32),
        VM((NC, 2, rows_dev, dim, length), F32),
        VM((NC, 2, rows_dev, dim, length), BF),
        VM((4, NC, rows_dev, dim, span // 4), F32),
        VM((NC, rows_dev, dim, span), BF),
        VM((2, rows_dev, dim, length), BF),
        VM((2, rows_dev, dim, length), BF),
        VM((2, nz, NY, NC) + tile, BF),
        VM((2, NY - 1, nz // 2, NC) + tile, BF),
        VM((2, nz - 1, NY // 2, NC) + tile, BF),
        VM((nz, NC) + tile, BF),
        VM((NY, NC) + tile, BF),
        VM((nz - 1, NC) + tile, BF),
        VM((NY - 1, NC) + tile, BF),
        VM((2, NC) + tile, F32),
        VM((NA * NX, 2, rows_dev, dim, block), BF),
        dma(4),
        dma(EXCHANGES),
        dma(EXCHANGES),
    ]
    passed = (
        jax.ShapeDtypeStruct((NX, rows_dev, dim, block), BF),
        jax.ShapeDtypeStruct((2, rows_dev, feature, block), BF),
        jax.ShapeDtypeStruct((heads,) + tile, F32),
    )
    parts = pl.pallas_call(
        lambda *refs: kernel(nz, *refs),
        out_shape=passed,
        in_specs=[pl.BlockSpec(memory_space=pltpu.SMEM)] + [vmem] * 5,
        out_specs=(vmem,) * 3,
        scratch_shapes=scratch,
        compiler_params=pltpu.CompilerParams(
            collective_id=0, has_side_effects=True, vmem_limit_bytes=60 * 1024 * 1024
        ),
        name="attention_grad",
    )(key_lengths, queries, keys_in, values, cotangent, pair_bias)
    return pl.pallas_call(
        lambda *refs: finish(nz, *refs),
        out_shape=(kind, kind, kind, jax.ShapeDtypeStruct(pair_bias.shape, F32)),
        in_specs=[vmem] * 3,
        out_specs=(vmem,) * 4,
        scratch_shapes=[VM((block, feature), BF)],
        compiler_params=pltpu.CompilerParams(vmem_limit_bytes=60 * 1024 * 1024),
        name="finish",
    )(*parts)


def solution(mesh):
    wide = P("row", "key", None)
    bias = P(None, ("key", "row"), None)
    return jax.shard_map(
        per_device,
        mesh=mesh,
        in_specs=(wide, wide, wide, wide, bias, P("row")),
        out_specs=(wide, wide, wide, bias),
        check_vma=False,
    )
```

time: 61.9 us -> 57.5 us (0.929)
  Pallas kernels: 61.1 us -> 56.7 us
    pallas_call x1, Pallas kernels: 59.2 us -> 54.8 us  [per_device(): pl.pallas_call(lambda *refs: kernel(nz, *refs), out_shape=passed, in_spec...]
where the time goes in v4:
time: 57.5 us; the launch traced here: 57.4 us
  Pallas kernels  56.7 us (99%)
  between operations  0.64 us (1%)
    pallas_call x1, Pallas kernels, per_device(): pl.pallas_call(lambda *refs: kernel(nz, *refs), out_shape=passed, in_spec...  54.8 us
    pallas_call x1, Pallas kernels, per_device(): pl.pallas_call(lambda *refs: finish(nz, *refs), out_shape=(kind, kind, ki...  1.92 us

profile of v4, /device:TPU:1, one launch (start us, length us, event | category | flops | bytes accessed | tf_op | source)
XLA Modules:
  0.0 57.4 jit_solution(6015680199285060670)
XLA Ops:
  0.6 54.8 %attention_grad.1 = (bf16[4,4,32,128]{3,2,1,0:T(8,128)(2,1)}, bf16[2,4,128,128]{3,2,1,0:T(8,128)(2,1)}, f32[4,16,128]{2,1,0:T(8,128)}) custom-call(s32[4]{0:T(128)} %refs_0_.1, bf16[4,128,128]{2,1,0:T(8,128)(2,1)} %refs_1_.1, bf16[4,128,128]{2,1,0:T(8,128)(2,1)} %refs_2_.1, bf16[4,128,128]{2,1,0:T(8,128)(2,1)} %refs_3_.1, bf16[4,128,128]{2,1,0:T(8,128)(2,1)} %refs_4_.1, ...), custom_call_target="tpu_custom_call" | custom-call | tf_op jit(solution)/shard_map/attention_grad/pallas_call | solution.py:494
  55.4 1.9 %finish.1 = (bf16[4,128,128]{2,1,0:T(8,128)(2,1)}, bf16[4,128,128]{2,1,0:T(8,128)(2,1)}, bf16[4,128,128]{2,1,0:T(8,128)(2,1)}, f32[4,2,1024]{2,1,0:T(2,128)}) custom-call(bf16[4,4,32,128]{3,2,1,0:T(8,128)(2,1)} %get-tuple-element.7.refs_0_, bf16[2,4,128,128]{3,2,1,0:T(8,128)(2,1)} %get-tuple-element.8.refs_1_, f32[4,16,128]{2,1,0:T(8,128)} %get-tuple-element.9.refs_2_), custom_call_target="tpu_custom_call" | custom-call | tf_op jit(solution)/shard_map/finish/pallas_call | solution.py:505

commit v5 on v4

--- a/solution.py
+++ b/solution.py
@@ -60,9 +60,10 @@
 
 
 def kernel(
-    nz, lengths, q, k, v, c, bias, rq, ks, r4,
+    nz, lengths, q_in, k_in, v_in, c_in, bias, oq, ok, ov, r4,
+    q, k, v, c, rq, done,
     pieces, own, bg, kvs, qcs, kv, qc, qs, lens, stage, eb, e, gws, total, acc, dkv, gqs, gq, rd,
-    sd, gbs, r2a, r2b, s2a, s2b, r3a, r3b, s3, rk, loc, out_sems, in_sems,
+    sd, gbs, r2a, r2b, s2a, s2b, r3a, r3b, r5, rk, loc, out_sems, in_sems,
 ):
     row, key, a, x, z, y, core = place()
     rows_dev, block, feature = q.shape
@@ -83,6 +84,12 @@
     def z_peer(s):
         return (row_of(lax.rem(z + s, nz), y, core), key)
 
+    loads = start(
+        [
+            pltpu.make_async_copy(there, held, loc.at[4 + n])
+            for n, (there, held) in enumerate(((k_in, k), (v_in, v), (q_in, q), (c_in, c)))
+        ]
+    )
     ys, zs, xs = far_first(NY), far_first(nz), far_first(NX)
     barrier = pltpu.get_barrier_semaphore()
     peers = [(row, lax.rem(key + s, NA * NX)) for s in range(1, NA * NX)]
@@ -90,6 +97,46 @@
     peers += [z_peer(s) for s in zs] + [y_peer(s) for s in ys]
     for peer in peers:
         pl.semaphore_signal(barrier, inc=1, device_id=peer, device_id_type=MESH)
+
+    def gatherers(even):
+        found = []
+        for s in zs + [0] if even else ys + [0]:
+            at = row_of(lax.rem(z + s, nz), y, half) if even else row_of(z, lax.rem(y + s, NY), half)
+            for t in [2, 1, 3, 0]:
+                to = lax.rem(x + t, NX)
+                found.append((s == 0 and t == 0, to, (at, a * NX + to)))
+        return found
+
+    def owners(even):
+        found = []
+        for s in zs + [0] if even else ys + [0]:
+            for g in range(NC):
+                if even:
+                    at, zy = row_of(lax.rem(z + s, nz), y, g), lax.rem(z + s, nz)
+                else:
+                    at, zy = row_of(z, lax.rem(y + s, NY), g), lax.rem(y + s, NY)
+                same = (core == g) & here & (side == (0 if even else 1))
+                found.append((s == 0, same, zy, g, (at, a * NX + core * 2 + (0 if even else 1))))
+        return found
+
+    def greet(peer):
+        pl.semaphore_signal(barrier, inc=1, device_id=peer, device_id_type=MESH)
+
+    for even in (True, False):
+
+        @pl.when(side == (0 if even else 1))
+        def _():
+            for maybe, _, peer in gatherers(even):
+                if maybe:
+                    pl.when(jnp.logical_not(here))(lambda: greet(peer))
+                else:
+                    greet(peer)
+
+        for maybe, same, _, _, peer in owners(even):
+            if maybe:
+                pl.when(jnp.logical_not(same))(lambda: greet(peer))
+            else:
+                greet(peer)
 
     for h in range(NX):
         lines = bias[h].astype(F32)
@@ -104,7 +151,8 @@
     for i in range(rows_dev):
         known = jnp.where(spots == i, lengths[i].astype(F32), known)
     lens[core] = known
-    pl.semaphore_wait(barrier, len(peers))
+    several = jnp.where(side == 0, NX * nz, NX * NY) + NC * (nz + NY)
+    pl.semaphore_wait(barrier, len(peers) + several - jnp.where(here, 2, 0))
 
     target = row_of(z, y, half)
 
@@ -132,6 +180,8 @@
         own[side, core] = pieces[x]
 
     tell = start([remote(lens.at[core], lens.at[core], mlen, (other, key))])
+    loads[0].wait()
+    loads[1].wait()
     for part, source in enumerate((k, v)):
         for i in range(rows_dev):
             turned = source[i].T
@@ -151,6 +201,8 @@
         [pltpu.make_async_copy(kvs.at[x], kv.at[core, :, :, :, pl.ds(key * 128, 128)], loc.at[0])]
     )
 
+    loads[2].wait()
+    loads[3].wait()
     for part, source in enumerate((q, c)):
         for i in range(rows_dev):
             lines = []
@@ -357,12 +409,15 @@
         for s in range(nz - 1):
             part += r2b[n, s].astype(F32)
         s2b[n * NY // 2 : (n + 1) * NY // 2] = part.astype(BF)
-    sum3b = start(
-        [
-            remote(s2b.at[lax.rem(y + s, NY)], r3b.at[s - 1], n3b, y_peer(s))
-            for s in ys
-        ]
-    )
+    def home(even, source):
+        for maybe, same, zy, g, peer in owners(even):
+            cp = remote(source.at[zy, g], r5.at[x * NY + (z if even else y)], n4, peer)
+            if maybe:
+                pl.when(jnp.logical_not(same))(cp.start)
+            else:
+                cp.start()
+
+    home(False, s2b)
     take(n2[0][1], r2a.at[0])
     take(n2[1][1], r2a.at[1])
     for n in range(2):
@@ -370,68 +425,60 @@
         for s in range(NY - 1):
             part += r2a[n, s].astype(F32)
         s2a[n * nz // 2 : (n + 1) * nz // 2] = part.astype(BF)
-    sum3a = start(
-        [
-            remote(s2a.at[lax.rem(z + s, nz)], r3a.at[s - 1], n3a, z_peer(s))
-            for s in zs
-        ]
-    )
-    take(n3a[1], r3a)
-    part = s2a[z].astype(F32)
-    for s in range(nz - 1):
-        part += r3a[s].astype(F32)
-    s3[0] = part
-    take(n3b[1], r3b)
-    part = s2b[y].astype(F32)
-    for s in range(NY - 1):
-        part += r3b[s].astype(F32)
-    s3[1] = part
-    for b in range(2):
-        for g in range(NC):
-            away = jnp.logical_not((x == core * 2 + b) & (core == g))
-            owner = (row_of(z, y, g), a * NX + core * 2 + b)
-            cp = remote(s3.at[b, g], r4.at[x], n4, owner)
-            pl.when(away)(cp.start)
-
-    @pl.when(here)
-    def _():
-        r4[x] = s3[side, core]
-
+    home(True, s2a)
+    pl.when(here & (side == 0))(lambda: r5.__setitem__(x * NY + z, s2a[z, core]))
+    pl.when(here & (side == 1))(lambda: r5.__setitem__(x * NY + y, s2b[y, core]))
     take(nkv[1], rk.at[0:7])
     held[0].wait()
     for i in range(rows_dev):
         for part in range(2):
-            for h in range(NX):
-                ks[part, i, h * dim : (h + 1) * dim] = (
-                    rk[h, part, i].astype(F32) + rk[NX + h, part, i].astype(F32)
-                ).astype(BF)
+            both = [
+                rk[h, part, i].astype(F32) + rk[NX + h, part, i].astype(F32) for h in range(NX)
+            ]
+            done[1 + part, i] = jnp.concatenate(both, axis=0).astype(BF).T
+    leaving = start([pltpu.make_async_copy(done.at[1], ok, loc.at[8]), pltpu.make_async_copy(done.at[2], ov, loc.at[9])])
     for away, keep in backs:
         pl.when(jnp.logical_not(away))(keep.wait)
     take_some(ngq[1], rq)
-    take_some(n4[1], r4)
+    for i in range(rows_dev):
+        turned = jnp.concatenate([rq[h, i] for h in range(NX)], axis=0).T
+        for n in range(2 * nz):
+            at = jnp.where(side == 1, (n % nz) * 2 + n // nz, n)
+            done[0, i, pl.ds(pl.multiple_of(at * 16, 16), 16)] = turned[n * 16 : (n + 1) * 16]
+    leaving += start([pltpu.make_async_copy(done.at[0], oq, loc.at[10])])
+    for even, count in ((True, nz), (False, NY)):
+
+        @pl.when(side == (0 if even else 1))
+        def _():
+            pl.when(here)(lambda: take(n4[1], r5.at[0 : NX * count - 1]))
+            pl.when(jnp.logical_not(here))(lambda: take(n4[1], r5.at[0 : NX * count]))
+            for h in range(NX):
+                part = r5[h * NY].astype(F32)
+                for n in range(1, count):
+                    part += r5[h * NY + n].astype(F32)
+                r4[h] = part
+
     take_some(m0[0], pieces)
     take_some(mqc[0], qcs)
     take_some(ngq[0], rq)
-    take_some(n4[0], r4)
+    pl.when(here)(lambda: take(n4[0], r5.at[0:23]))
+    pl.when(jnp.logical_not(here))(lambda: take(n4[0], r5.at[0:24]))
     for group, like in (
-        (m1a, r3a), (m1b, r3b), (n3a, r3a), (n3b, r3b), (mkv, rk.at[0:7]), (nkv, rk.at[0:7]),
+        (m1a, r3a), (m1b, r3b), (mkv, rk.at[0:7]), (nkv, rk.at[0:7]),
         (mswap, rd), (nswap, rd), (mlen, lens.at[0]),
     ):
         take(group[0], like)
     for group in (m2, n2):
         for n in range(4):
             take(group[n][0], r2a.at[0] if n < 2 else r2b.at[0])
-
-
-def finish(nz, rq, ks, r4, oq, ok, ov, ob, held):
-    odd = lax.rem(lax.axis_index("key"), 2)
-    for i in range(oq.shape[0]):
-        held[...] = jnp.concatenate([rq[h, i] for h in range(NX)], axis=0).T
-        for n in range(2 * nz):
-            at = jnp.where(odd == 1, (n % 2) * nz + n // 2, n)
-            oq[i, n * 16 : (n + 1) * 16] = held[pl.ds(pl.multiple_of(at * 16, 16), 16)]
-        ok[i] = ks[0, i].T
-        ov[i] = ks[1, i].T
+    for cp in leaving:
+        cp.wait()
+
+
+def finish(q_in, k_in, v_in, r4, oq, ok, ov, ob):
+    oq[...] = q_in[...]
+    ok[...] = k_in[...]
+    ov[...] = v_in[...]
     for h in range(NX):
         for j in range(2):
             for t in range(8):
@@ -453,6 +500,12 @@
     vmem = pl.BlockSpec(memory_space=VM)
     kind = jax.ShapeDtypeStruct(queries.shape, BF)
     scratch = [
+        VM(queries.shape, BF),
+        VM(queries.shape, BF),
+        VM(queries.shape, BF),
+        VM(queries.shape, BF),
+        VM((NX, rows_dev, dim, block), BF),
+        VM((3,) + queries.shape, BF),
         VM((NX,) + tile, BF),
         VM((2, NC) + tile, BF),
         VM((2, nz, NY, NC) + tile, BF),
@@ -480,22 +533,19 @@
         VM((NY, NC) + tile, BF),
         VM((nz - 1, NC) + tile, BF),
         VM((NY - 1, NC) + tile, BF),
-        VM((2, NC) + tile, F32),
+        VM((NX * NY,) + tile, BF),
         VM((NA * NX, 2, rows_dev, dim, block), BF),
-        dma(4),
+        dma(11),
         dma(EXCHANGES),
         dma(EXCHANGES),
     ]
-    passed = (
-        jax.ShapeDtypeStruct((NX, rows_dev, dim, block), BF),
-        jax.ShapeDtypeStruct((2, rows_dev, feature, block), BF),
-        jax.ShapeDtypeStruct((heads,) + tile, F32),
-    )
+    passed = (kind, kind, kind, jax.ShapeDtypeStruct((heads,) + tile, F32))
+    away = pl.BlockSpec(memory_space=pl.ANY)
     parts = pl.pallas_call(
         lambda *refs: kernel(nz, *refs),
         out_shape=passed,
-        in_specs=[pl.BlockSpec(memory_space=pltpu.SMEM)] + [vmem] * 5,
-        out_specs=(vmem,) * 3,
+        in_specs=[pl.BlockSpec(memory_space=pltpu.SMEM)] + [away] * 4 + [vmem],
+        out_specs=(away,) * 3 + (vmem,),
         scratch_shapes=scratch,
         compiler_params=pltpu.CompilerParams(
             collective_id=0, has_side_effects=True, vmem_limit_bytes=60 * 1024 * 1024
@@ -503,11 +553,10 @@
         name="attention_grad",
     )(key_lengths, queries, keys_in, values, cotangent, pair_bias)
     return pl.pallas_call(
-        lambda *refs: finish(nz, *refs),
+        finish,
         out_shape=(kind, kind, kind, jax.ShapeDtypeStruct(pair_bias.shape, F32)),
-        in_specs=[vmem] * 3,
+        in_specs=[vmem] * 4,
         out_specs=(vmem,) * 4,
-        scratch_shapes=[VM((block, feature), BF)],
         compiler_params=pltpu.CompilerParams(vmem_limit_bytes=60 * 1024 * 1024),
         name="finish",
     )(*parts)

time: 57.5 us -> 56 us (0.974)
  Pallas kernels: 56.7 us -> 55.2 us
    pallas_call x1, Pallas kernels: 54.8 us -> 53.4 us  [per_device(): pl.pallas_call(lambda *refs: kernel(nz, *refs), out_shape=passed, in_spec...]
where the time goes in v5:
time: 56 us; the launch traced here: 55.8 us
  Pallas kernels  55.2 us (99%)
  between operations  0.64 us (1%)
    pallas_call x1, Pallas kernels, per_device(): pl.pallas_call(lambda *refs: kernel(nz, *refs), out_shape=passed, in_spec...  53.4 us
    pallas_call x1, Pallas kernels, per_device(): pl.pallas_call(finish, out_shape=(kind, kind, kind, jax.ShapeDtypeStruct(...  1.79 us

profile of v5, /device:TPU:1, one launch (start us, length us, event | category | flops | bytes accessed | tf_op | source)
XLA Modules:
  0.0 55.8 jit_solution(15860787080903325337)
XLA Ops:
  0.6 53.4 %attention_grad.1 = (bf16[4,128,128]{2,1,0:T(8,128)(2,1)}, bf16[4,128,128]{2,1,0:T(8,128)(2,1)}, bf16[4,128,128]{2,1,0:T(8,128)(2,1)}, f32[4,16,128]{2,1,0:T(8,128)}) custom-call(s32[4]{0:T(128)} %refs_0_.1, bf16[4,128,128]{2,1,0:T(8,128)(2,1)} %refs_1_.1, bf16[4,128,128]{2,1,0:T(8,128)(2,1)} %refs_2_.1, bf16[4,128,128]{2,1,0:T(8,128)(2,1)} %refs_3_.1, ...), custom_call_target="tpu_custom_call" | custom-call | tf_op jit(solution)/shard_map/attention_grad/pallas_call | solution.py:544
  54.0 1.8 %finish.1 = (bf16[4,128,128]{2,1,0:T(8,128)(2,1)}, bf16[4,128,128]{2,1,0:T(8,128)(2,1)}, bf16[4,128,128]{2,1,0:T(8,128)(2,1)}, f32[4,2,1024]{2,1,0:T(2,128)}) custom-call(bf16[4,128,128]{2,1,0:T(8,128)(2,1)} %get-tuple-element.8.q_in, bf16[4,128,128]{2,1,0:T(8,128)(2,1)} %get-tuple-element.9.k_in, bf16[4,128,128]{2,1,0:T(8,128)(2,1)} %get-tuple-element.10.v_in, ...), custom_call_target="tpu_custom_call" | custom-call | tf_op jit(solution)/shard_map/finish/pallas_call | solution.py:555

commit v6 on v5

--- a/solution.py
+++ b/solution.py
@@ -132,11 +132,6 @@
                 else:
                     greet(peer)
 
-        for maybe, same, _, _, peer in owners(even):
-            if maybe:
-                pl.when(jnp.logical_not(same))(lambda: greet(peer))
-            else:
-                greet(peer)
 
     for h in range(NX):
         lines = bias[h].astype(F32)
@@ -151,8 +146,7 @@
     for i in range(rows_dev):
         known = jnp.where(spots == i, lengths[i].astype(F32), known)
     lens[core] = known
-    several = jnp.where(side == 0, NX * nz, NX * NY) + NC * (nz + NY)
-    pl.semaphore_wait(barrier, len(peers) + several - jnp.where(here, 2, 0))
+    pl.semaphore_wait(barrier, len(peers) + NC * (nz + NY) - jnp.where(here, 1, 0))
 
     target = row_of(z, y, half)
 

time: 56 us -> 56.6 us (1.011)
  Pallas kernels: 55.2 us -> 55.8 us
where the time goes in v6:
time: 56.6 us; the launch traced here: 56.4 us
  Pallas kernels  55.8 us (99%)
  between operations  0.64 us (1%)
    pallas_call x1, Pallas kernels, per_device(): pl.pallas_call(lambda *refs: kernel(nz, *refs), out_shape=passed, in_spec...  54 us
    pallas_call x1, Pallas kernels, per_device(): pl.pallas_call(finish, out_shape=(kind, kind, kind, jax.ShapeDtypeStruct(...  1.79 us

profile of v6, /device:TPU:1, one launch (start us, length us, event | category | flops | bytes accessed | tf_op | source)
XLA Modules:
  0.0 56.4 jit_solution(11078702250589084596)
XLA Ops:
  0.6 54.0 %attention_grad.1 = (bf16[4,128,128]{2,1,0:T(8,128)(2,1)}, bf16[4,128,128]{2,1,0:T(8,128)(2,1)}, bf16[4,128,128]{2,1,0:T(8,128)(2,1)}, f32[4,16,128]{2,1,0:T(8,128)}) custom-call(s32[4]{0:T(128)} %refs_0_.1, bf16[4,128,128]{2,1,0:T(8,128)(2,1)} %refs_1_.1, bf16[4,128,128]{2,1,0:T(8,128)(2,1)} %refs_2_.1, bf16[4,128,128]{2,1,0:T(8,128)(2,1)} %refs_3_.1, ...), custom_call_target="tpu_custom_call" | custom-call | tf_op jit(solution)/shard_map/attention_grad/pallas_call | solution.py:538
  54.6 1.8 %finish.1 = (bf16[4,128,128]{2,1,0:T(8,128)(2,1)}, bf16[4,128,128]{2,1,0:T(8,128)(2,1)}, bf16[4,128,128]{2,1,0:T(8,128)(2,1)}, f32[4,2,1024]{2,1,0:T(2,128)}) custom-call(bf16[4,128,128]{2,1,0:T(8,128)(2,1)} %get-tuple-element.8.q_in, bf16[4,128,128]{2,1,0:T(8,128)(2,1)} %get-tuple-element.9.k_in, bf16[4,128,128]{2,1,0:T(8,128)(2,1)} %get-tuple-element.10.v_in, ...), custom_call_target="tpu_custom_call" | custom-call | tf_op jit(solution)/shard_map/finish/pallas_call | solution.py:549
